TPU v7x, 512 devices: a whole 4x4x16 slice. The times are simulated.
512 devices in a mesh: tm: 128 (over z, y, x_lo), head: 4 (over x_hi, core).
Axes of the slice: x: 4 (x_hi: 2, x_lo: 2; x = x_hi * 2 + x_lo), y: 4, z: 16, core: 2. Of those that a mesh axis runs over, the one named last changes fastest.
Arguments:
- q_video: bfloat16 [65536, 3072], P('tm', 'head')
- k_video: bfloat16 [65536, 3072], P('tm', 'head')
- v_video: bfloat16 [65536, 3072], P('tm', 'head'), may hold values from -6 to 6
- q_audio: bfloat16 [32768, 3072], P('tm', 'head')
- k_audio: bfloat16 [32768, 3072], P('tm', 'head')
- v_audio: bfloat16 [32768, 3072], P('tm', 'head'), may hold values from -6 to 6
- q_gain_video: float32 [3072], P('head'), may hold values from 0.1 to 1.9
- k_gain_video: float32 [3072], P('head'), may hold values from 0.1 to 1.9
- q_gain_audio: float32 [3072], P('head'), may hold values from 0.1 to 1.9
- k_gain_audio: float32 [3072], P('head'), may hold values from 0.1 to 1.9
- audio_align: int32 [32768], P('tm'), may hold values from 0 to 65535, as said below
- windows: int32 [2, 24], P(None, 'head'), may hold values from 32 to 128
Outputs:
- video_out: bfloat16 [65536, 3072], P('tm', 'head')
- audio_out: bfloat16 [32768, 3072], P('tm', 'head')
Inputs may be any that keep to these rules, and one draw needn't show every extreme that they name: audio_align[j] equals 2 j plus an offset of 0 to 48, cut at 65535; it is 0 at j = 0 and 65535 at the last audio token.
All inputs are finite; a program needn't handle non-finite values.
Results may differ from a plain program's by a relative error of at most 0.0096.
Values may be sent and summed in bfloat16 or wider, within the bound.
A program may use at most 64 MiB of HBM per device.

v0:
```python
import jax
import jax.numpy as jnp
from jax import lax
from jax.sharding import PartitionSpec as P

HEAD_DIM = 128
D = 3072
WINDOW_REACH = 128
WC = 64
DRIFT = 48


EPS = 1e-06


def extended(array, sides, width):
    for axis, dim in sides:
        size, length = (lax.axis_size(axis), array.shape[dim])
        up = [(i, (i + 1) % size) for i in range(size - 1)]
        down = [(j, i) for i, j in up]
        last = lax.slice_in_dim(array, length - width, length, axis=dim)
        leading = lax.slice_in_dim(array, 0, width, axis=dim)
        before = lax.ppermute(last, axis, up)
        after = lax.ppermute(leading, axis, down)
        array = jnp.concatenate([before, array, after], axis=dim)
    return array


def squares(values):
    wide = values.astype(jnp.float32)
    return jnp.sum(wide * wide, axis=1)


def apply_norm(values, factor, gain):
    return (values.astype(jnp.float32) * factor[:, None] * gain).astype(jnp.bfloat16)


def compute_block_attention(query, keys, values, mask):
    scores = jnp.einsum("rhe,khe->hrk", query, keys, preferred_element_type=jnp.float32)
    scores = scores * (1.0 / HEAD_DIM**0.5)
    scores = jnp.where(mask, scores, -1e30)
    top = jnp.max(scores, axis=-1, keepdims=True)
    expo = jnp.exp(scores - top)
    probs = (expo / jnp.sum(expo, axis=-1, keepdims=True)).astype(jnp.bfloat16)
    return jnp.einsum("hrk,khe->rhe", probs, values, preferred_element_type=jnp.float32)


def body(
    q_video,
    k_video,
    v_video,
    q_audio,
    k_audio,
    v_audio,
    q_gain_video,
    k_gain_video,
    q_gain_audio,
    k_gain_audio,
    audio_align,
    windows,
):
    rows_v, cols = q_video.shape
    rows_a = q_audio.shape[0]
    parts = cols // HEAD_DIM
    sums = lax.psum(
        (squares(q_video), squares(k_video), squares(q_audio), squares(k_audio)), "head"
    )
    fqv, fkv, fqa, fka = [lax.rsqrt(total / D + EPS) for total in sums]
    qv = apply_norm(q_video, fqv, q_gain_video)
    qa = apply_norm(q_audio, fqa, q_gain_audio)
    kv_local = apply_norm(k_video, fkv, k_gain_video)
    ka_local = apply_norm(k_audio, fka, k_gain_audio)
    kv_wide, vv_wide = (
        extended(kv_local, (("tm", 0),), WINDOW_REACH),
        extended(v_video, (("tm", 0),), WINDOW_REACH),
    )
    ka_wide, va_wide, align_wide = (
        extended(ka_local, (("tm", 0),), WINDOW_REACH),
        extended(v_audio, (("tm", 0),), WINDOW_REACH),
        extended(audio_align, (("tm", 0),), WINDOW_REACH),
    )
    place = lax.axis_index("tm")
    count = lax.axis_size("tm")
    total_v = rows_v * count
    total_a = rows_a * count
    qv3 = qv.reshape(rows_v, parts, HEAD_DIM)
    qa3 = qa.reshape(rows_a, parts, HEAD_DIM)
    kv3 = kv_wide.reshape(rows_v + 2 * WINDOW_REACH, parts, HEAD_DIM)
    vv3 = vv_wide.reshape(rows_v + 2 * WINDOW_REACH, parts, HEAD_DIM)
    ka3 = ka_wide.reshape(rows_a + 2 * WINDOW_REACH, parts, HEAD_DIM)
    audio_value_split = va_wide.reshape(rows_a + 2 * WINDOW_REACH, parts, HEAD_DIM)
    win_video = windows[0][:, None, None]
    win_audio = windows[1][:, None, None]
    block_v = min(128, rows_v)
    audio_block_rows = block_v // 2
    blocks = rows_v // block_v
    reach = (WC + DRIFT + 1) // 2
    video_blocks = []
    audio_blocks = []
    for blk in range(blocks):
        v0 = blk * block_v
        audio_first_row = blk * audio_block_rows
        qpos = place * rows_v + v0 + jnp.arange(block_v, dtype=jnp.int32)
        aqpos = place * rows_a + audio_first_row + jnp.arange(audio_block_rows, dtype=jnp.int32)
        vkpos = (
            place * rows_v
            + v0
            - WINDOW_REACH
            + jnp.arange(block_v + 2 * WINDOW_REACH, dtype=jnp.int32)
        )
        vkval = (vkpos >= 0) & (vkpos < total_v)
        akpos = (
            place * rows_a
            + audio_first_row
            - WINDOW_REACH
            + jnp.arange(audio_block_rows + 2 * WINDOW_REACH, dtype=jnp.int32)
        )
        akval = (akpos >= 0) & (akpos < total_a)
        cstart = audio_first_row + WINDOW_REACH - reach
        clen = audio_block_rows + 2 * reach
        ckpos = place * rows_a + audio_first_row - reach + jnp.arange(clen, dtype=jnp.int32)
        ckval = (ckpos >= 0) & (ckpos < total_a)
        calign = align_wide[cstart : cstart + clen]
        arows_align = audio_align[audio_first_row : audio_first_row + audio_block_rows]
        video_self_output = (jnp.abs(qpos[:, None] - vkpos[None, :])[None] <= win_video) & vkval[
            None, None, :
        ]
        video_cross_output = ((jnp.abs(calign[None, :] - qpos[:, None]) <= WC) & ckval[None, :])[
            None
        ]
        audio_self_output = (jnp.abs(aqpos[:, None] - akpos[None, :])[None] <= win_audio) & akval[
            None, None, :
        ]
        audio_cross_output = (
            (jnp.abs(arows_align[:, None] - vkpos[None, :]) <= WC) & vkval[None, :]
        )[None]
        video_query_block = qv3[v0 : v0 + block_v]
        audio_query_block = qa3[audio_first_row : audio_first_row + audio_block_rows]
        video_key_block = kv3[v0 : v0 + block_v + 2 * WINDOW_REACH]
        video_value_block = vv3[v0 : v0 + block_v + 2 * WINDOW_REACH]
        audio_key_block = ka3[
            audio_first_row : audio_first_row + audio_block_rows + 2 * WINDOW_REACH
        ]
        audio_value_block = audio_value_split[
            audio_first_row : audio_first_row + audio_block_rows + 2 * WINDOW_REACH
        ]
        kac = ka3[cstart : cstart + clen]
        vac = audio_value_split[cstart : cstart + clen]
        video_tokens = compute_block_attention(
            video_query_block, video_key_block, video_value_block, video_self_output
        ) + compute_block_attention(video_query_block, kac, vac, video_cross_output)
        audio_tokens = compute_block_attention(
            audio_query_block, audio_key_block, audio_value_block, audio_self_output
        ) + compute_block_attention(
            audio_query_block, video_key_block, video_value_block, audio_cross_output
        )
        video_blocks.append(video_tokens.reshape(block_v, cols).astype(jnp.bfloat16))
        audio_blocks.append(audio_tokens.reshape(audio_block_rows, cols).astype(jnp.bfloat16))
    return (jnp.concatenate(video_blocks, axis=0), jnp.concatenate(audio_blocks, axis=0))


def solution(mesh):
    placed = (
        P("tm", "head"),
        P("tm", "head"),
        P("tm", "head"),
        P("tm", "head"),
        P("tm", "head"),
        P("tm", "head"),
        P("head"),
        P("head"),
        P("head"),
        P("head"),
        P("tm"),
        P(None, "head"),
    )
    return jax.shard_map(
        body,
        mesh=mesh,
        in_specs=placed,
        out_specs=(P("tm", "head"), P("tm", "head")),
        check_vma=False,
    )
```

profile of v0, /device:TPU:256, one launch (start us, length us, event | category | flops | bytes accessed | tf_op | source)
XLA Modules:
  0.0 198.2 jit_solution(3079242079878489479)
XLA Ops:
  4.4 10.1 %all-reduce = (f32[512]{0:T(512)S(1)}, f32[256]{0:T(256)S(1)}, f32[512]{0:T(512)S(1)}, f32[256]{0:T(256)S(1)}) all-reduce(f32[512]{0:T(512)S(1)} %fusion.16, f32[256]{0:T(256)S(1)} %fusion.84, f32[512]{0:T(512)S(1)} %fusion.19, f32[256]{0:T(256)S(1)} %fusion.87), channel_id=1, replica_groups=mesh['tm'=128,'head'=4] {'head'}, use_global_device_ids=true, to_apply=%region_1.0 | all-reduce | flops 1536 | bytes 12288 | tf_op jit(solution)/shard_map/psum | solution.py:65
  15.9 2.6 %collective-permute-start.4 = (bf16[128,768]{1,0:T(8,128)(2,1)}, bf16[128,768]{1,0:T(8,128)(2,1)}, u32[]{:S(2)}, u32[]{:S(2)}) collective-permute-start(bf16[128,768]{1,0:T(8,128)(2,1)} %get-tuple-element.40), channel_id=1, source_target_pairs={{0,4},{4,8},{8,12},{12,16},{16,20},{20,24},{24,28},{28,32},{32,36}... | collective-permute-start | bytes 589832 | tf_op jit(solution)/shard_map/ppermute | solution.py:23
  18.6 7.6 %collective-permute-start.9 = (bf16[128,768]{1,0:T(8,128)(2,1)}, bf16[128,768]{1,0:T(8,128)(2,1)}, u32[]{:S(2)}, u32[]{:S(2)}) collective-permute-start(bf16[128,768]{1,0:T(8,128)(2,1)} %get-tuple-element.41), channel_id=1, source_target_pairs={{4,0},{8,4},{12,8},{16,12},{20,16},{24,20},{28,24},{32,28},{36,32}... | collective-permute-start | bytes 589832 | tf_op jit(solution)/shard_map/ppermute | solution.py:24
  26.7 1.9 collective-permute-start.3
  28.7 8.1 %collective-permute-start.8 = (s32[128]{0:T(128)}, s32[128]{0:T(128)}, u32[]{:S(2)}, u32[]{:S(2)}) collective-permute-start(s32[128]{0:T(128)} %get-tuple-element.57), channel_id=1, source_target_pairs={{4,0},{8,4},{12,8},{16,12},{20,16},{24,20},{28,24},{32,28},{36,32}... | collective-permute-start | bytes 1544 | tf_op jit(solution)/shard_map/ppermute | solution.py:24
  66.4 8.1 %collective-permute-start.7 = (bf16[128,768]{1,0:T(8,128)(2,1)}, bf16[128,768]{1,0:T(8,128)(2,1)}, u32[]{:S(2)}, u32[]{:S(2)}) collective-permute-start(bf16[128,768]{1,0:T(8,128)(2,1)} %get-tuple-element.45), channel_id=1, source_target_pairs={{4,0},{8,4},{12,8},{16,12},{20,16},{24,20},{28,24},{32,28},{36,32}... | collective-permute-start | bytes 589832 | tf_op jit(solution)/shard_map/ppermute | solution.py:24
  74.6 1.9 collective-permute-start
  80.1 8.1 %collective-permute-start.6 = (bf16[128,768]{0,1:T(8,128)(2,1)S(1)}, bf16[128,768]{0,1:T(8,128)(2,1)S(1)}, u32[]{:S(2)}, u32[]{:S(2)}) collective-permute-start(bf16[128,768]{0,1:T(8,128)(2,1)S(1)} %get-tuple-element.11), channel_id=1, source_target_pairs={{4,0},{8,4},{12,8},{16,12},{20,16},{24,20},{28,24},{32,28},{36,32}... | collective-permute-start | bytes 589832 | tf_op jit(solution)/shard_map/ppermute | solution.py:24
  91.6 4.1 %collective-permute-start.5 = (bf16[128,768]{1,0:T(8,128)(2,1)}, bf16[128,768]{1,0:T(8,128)(2,1)}, u32[]{:S(2)}, u32[]{:S(2)}) collective-permute-start(bf16[128,768]{1,0:T(8,128)(2,1)} %get-tuple-element.17), channel_id=1, source_target_pairs={{4,0},{8,4},{12,8},{16,12},{20,16},{24,20},{28,24},{32,28},{36,32}... | collective-permute-start | bytes 589832 | tf_op jit(solution)/shard_map/ppermute | solution.py:24
  97.0 2.5 %fusion.205 = f32[6,128]{1,0:T(8,128)} fusion(bf16[128,6,128]{0,2,1:T(8,128)(2,1)} %bitcast.264, bf16[384,6,128]{0,2,1:T(8,128)(2,1)} %bitcast.243, s32[128,384]{1,0:T(8,128)} %subtract_abs_fusion, pred[384]{0:T(512)(128)(4,1)S(1)} %copy-done.78, s32[6]{0:T(128)S(1)} %copy-done.52), kind=kOutput, calls=%fused_computation.331 | convolution fusion | flops 77267328 | bytes 986520 | tf_op jit(solution)/shard_map/sub | solution.py:43
  101.0 1.9 fusion.206
  103.0 2.0 %fusion.67 = f32[6,128,176]{1,2,0:T(8,128)} fusion(bf16[128,6,128]{0,2,1:T(8,128)(2,1)S(1)} %bitcast.261, bf16[22,6,8,128]{3,2,1,0:T(8,128)(2,1)} %get-tuple-element.38, pred[128,176]{0,1:T(8,128)(4,1)S(1)} %copy-done.48), kind=kOutput, calls=%fused_computation.85 | convolution fusion | flops 34873344 | bytes 1030144 | tf_op jit(solution)/shard_map/rhe,khe->hrk/dot_general | solution.py:39
  105.0 1.9 fusion.210
  109.6 2.2 %fusion.69 = f32[6,128,176]{1,2,0:T(8,128)} fusion(bf16[128,6,128]{0,2,1:T(8,128)(2,1)} %bitcast.251, bf16[22,6,8,128]{3,2,1,0:T(8,128)(2,1)} %get-tuple-element.36, pred[128,176]{0,1:T(8,128)(4,1)} %fusion.140), kind=kOutput, calls=%fused_computation.89 | convolution fusion | flops 34873344 | bytes 1030144 | tf_op jit(solution)/shard_map/rhe,khe->hrk/dot_general | solution.py:39
  111.8 2.5 %fusion.32 = f32[6,128,384]{2,1,0:T(8,128)} fusion(bf16[128,6,128]{0,2,1:T(8,128)(2,1)} %bitcast.258, bf16[384,6,128]{0,2,1:T(8,128)(2,1)S(1)} %bitcast.240, s32[128,384]{1,0:T(8,128)} %subtract_abs_fusion.1, pred[384]{0:T(512)(128)(4,1)S(1)} %copy-done.76, s32[6]{0:T(128)S(1)} %copy-done.52), kind=kOutput, calls=%fused_computation.40 | convolution fusion | flops 76677120 | bytes 2163096 | tf_op jit(solution)/shard_map/rhe,khe->hrk/dot_general | solution.py:39
  114.3 2.3 %fusion.209 = f32[6,128]{1,0:T(8,128)} fusion(bf16[128,6,128]{0,2,1:T(8,128)(2,1)} %bitcast.259, bf16[384,6,128]{0,2,1:T(8,128)(2,1)S(1)} %bitcast.241, s32[128,384]{1,0:T(8,128)} %subtract_abs_fusion.1, pred[384]{0:T(512)(128)(4,1)S(1)} %copy-done.76, s32[6]{0:T(128)S(1)} %copy-done.52), kind=kOutput, calls=%fused_computation.333 | convolution fusion | flops 77267328 | bytes 986520 | tf_op jit(solution)/shard_map/sub | solution.py:43
  118.3 1.9 constant_dynamic-update-slice_fusion
  121.7 2.3 %fusion.213 = f32[6,128]{1,0:T(8,128)} fusion(bf16[128,6,128]{0,2,1:T(8,128)(2,1)} %bitcast.254, bf16[384,6,128]{0,2,1:T(8,128)(2,1)S(1)} %bitcast.238, s32[128,384]{1,0:T(8,128)} %subtract_abs_fusion.2, pred[384]{0:T(512)(128)(4,1)S(1)} %copy-done.74, s32[6]{0:T(128)S(1)} %copy-done.52), kind=kOutput, calls=%fused_computation.335 | convolution fusion | flops 77267328 | bytes 986520 | tf_op jit(solution)/shard_map/sub | solution.py:43
  124.0 2.5 %pad_maximum_fusion.4 = (bf16[384,768]{1,0:T(8,128)(2,1)}, bf16[384,768]{1,0:T(8,128)(2,1)}, bf16[384,768]{1,0:T(8,128)(2,1)}, bf16[384,768]{1,0:T(8,128)(2,1)}) fusion(bf16[512,768]{1,0:T(8,128)(2,1)S(1)} %copy-done, bf16[128,768]{1,0:T(8,128)(2,1)} %collective-permute-done, bf16[128,768]{1,0:T(8,128)(2,1)} %collective-permute-done.5), kind=kLoop, calls=%fused_computation.140 | loop fusion | flops 2359296 | bytes 4718592 | tf_op jit(solution)/shard_map/concatenate | solution.py:25
  126.5 2.2 %copy.46 = bf16[384,768]{0,1:T(8,128)(2,1)} copy(bf16[384,768]{1,0:T(8,128)(2,1)} %get-tuple-element.15) | data formatting | bytes 1179648 | tf_op jit(solution)/shard_map/slice | solution.py:140
  130.1 2.3 %fusion.217 = f32[6,128]{1,0:T(8,128)} fusion(bf16[128,6,128]{0,2,1:T(8,128)(2,1)S(1)} %bitcast.253, bf16[384,6,128]{0,2,1:T(8,128)(2,1)S(1)} %bitcast.235, s32[128,384]{1,0:T(8,128)} %subtract_abs_fusion.3, pred[384]{0:T(512)(128)(4,1)S(1)} %copy-done.72, s32[6]{0:T(128)S(1)} %copy-done.52), kind=kOutput, calls=%fused_computation.337 | convolution fusion | flops 77267328 | bytes 986520 | tf_op jit(solution)/shard_map/sub | solution.py:43
  134.4 2.3 %fusion.110 = f32[6,128,128]{2,1,0:T(8,128)} fusion(f32[6,128]{1,0:T(8,128)S(1)} %fusion.202, f32[6,128,176]{1,2,0:T(8,128)} %fusion.66, bf16[384,768]{1,0:T(8,128)(2,1)S(1)} %constant_dynamic-update-slice_fusion.2), kind=kOutput, calls=%fused_computation.176 | convolution fusion | flops 35009456 | bytes 1748992 | tf_op jit(solution)/shard_map/hrk,khe->rhe/dot_general | solution.py:45
  136.7 3.5 %fusion.73 = bf16[6,128,128]{2,1,0:T(8,128)(2,1)S(1)} fusion(f32[6,128,128]{2,1,0:T(8,128)} %fusion.110, bf16[384,6,128]{0,2,1:T(8,128)(2,1)} %bitcast.272, f32[6,128]{1,0:T(8,128)S(1)} %copy-done.90, f32[6,128,384]{2,1,0:T(8,128)} %fusion.33), kind=kOutput, calls=%fused_computation.101 | convolution fusion | flops 76579968 | bytes 2362368 | tf_op jit(solution)/shard_map/hrk,khe->rhe/dot_general | solution.py:45
  142.1 2.4 %fusion.113 = f32[6,128,128]{1,2,0:T(8,128)} fusion(bf16[22,6,8,128]{3,2,1,0:T(8,128)(2,1)} %get-tuple-element.47, f32[6,128]{1,0:T(8,128)S(1)} %copy-done.89, f32[6,128,176]{1,2,0:T(8,128)} %fusion.67), kind=kOutput, calls=%fused_computation.179 | convolution fusion | flops 35009456 | bytes 1207296 | tf_op jit(solution)/shard_map/hrk,khe->rhe/dot_general | solution.py:45
  144.5 3.5 %fusion.72 = bf16[6,128,128]{1,2,0:T(8,128)(2,1)S(1)} fusion(f32[6,128,128]{1,2,0:T(8,128)} %fusion.113, bf16[384,6,128]{0,2,1:T(8,128)(2,1)} %bitcast.270, f32[6,128]{1,0:T(8,128)S(1)} %copy-done.91, f32[6,128,384]{2,1,0:T(8,128)} %fusion.32), kind=kOutput, calls=%fused_computation.100 | convolution fusion | flops 76579968 | bytes 2362368 | tf_op jit(solution)/shard_map/hrk,khe->rhe/dot_general | solution.py:45
  150.0 2.4 %fusion.118 = f32[6,128,128]{1,2,0:T(8,128)} fusion(bf16[22,6,8,128]{3,2,1,0:T(8,128)(2,1)} %get-tuple-element.46, f32[6,128]{1,0:T(8,128)S(1)} %copy-done.88, f32[6,128,176]{1,2,0:T(8,128)} %fusion.68), kind=kOutput, calls=%fused_computation.184 | convolution fusion | flops 35009456 | bytes 1207296 | tf_op jit(solution)/shard_map/hrk,khe->rhe/dot_general | solution.py:45
  152.4 3.5 %fusion.71 = bf16[6,128,128]{1,2,0:T(8,128)(2,1)S(1)} fusion(f32[6,128,128]{1,2,0:T(8,128)} %fusion.118, bf16[384,6,128]{0,2,1:T(8,128)(2,1)} %bitcast.268, f32[6,128]{1,0:T(8,128)S(1)} %copy-done.92, f32[6,128,384]{2,1,0:T(8,128)} %fusion.31), kind=kOutput, calls=%fused_computation.99 | convolution fusion | flops 76579968 | bytes 2362368 | tf_op jit(solution)/shard_map/hrk,khe->rhe/dot_general | solution.py:45
  157.8 2.2 %fusion.195 = (bf16[320,768]{1,0:T(8,128)(2,1)}, bf16[320,768]{1,0:T(8,128)(2,1)}) fusion(bf16[384,768]{1,0:T(8,128)(2,1)} %get-tuple-element.42), kind=kLoop, calls=%fused_computation.323 | loop fusion | bytes 1966080 | tf_op jit(solution)/shard_map/slice | solution.py:144
  160.0 2.7 %fusion.125 = f32[6,128,128]{2,1,0:T(8,128)} fusion(f32[6,128]{1,0:T(8,128)S(1)} %fusion.214, f32[6,128,176]{1,2,0:T(8,128)} %fusion.69, bf16[384,768]{1,0:T(8,128)(2,1)} %get-tuple-element.42), kind=kOutput, calls=%fused_computation.191 | convolution fusion | flops 35009456 | bytes 1747968 | tf_op jit(solution)/shard_map/hrk,khe->rhe/dot_general | solution.py:45
  162.7 4.0 %fusion.70 = bf16[6,128,128]{2,1,0:T(8,128)(2,1)} fusion(f32[6,128,128]{2,1,0:T(8,128)} %fusion.125, bf16[384,6,128]{0,2,1:T(8,128)(2,1)S(1)} %bitcast.266, f32[6,128]{1,0:T(8,128)S(1)} %copy-done.93, f32[6,128,384]{2,1,0:T(8,128)} %fusion.30), kind=kOutput, calls=%fused_computation.98 | convolution fusion | flops 76579968 | bytes 2362368 | tf_op jit(solution)/shard_map/hrk,khe->rhe/dot_general | solution.py:45
  168.9 2.6 %fusion.103 = f32[6,128,64]{1,2,0:T(8,128)} fusion(bf16[384,6,128]{0,2,1:T(8,128)(2,1)} %bitcast.273, f32[6,64]{1,0:T(8,128)S(1)} %fusion.218, f32[6,64,384]{2,1,0:T(8,128)S(1)} %fusion.54), kind=kOutput, calls=%fused_computation.169 | convolution fusion | flops 38191872 | bytes 1377792 | tf_op jit(solution)/shard_map/hrk,khe->rhe/dot_general | solution.py:45
  172.5 2.3 %fusion.95 = (bf16[320,768]{1,0:T(8,128)(2,1)}, bf16[320,768]{1,0:T(8,128)(2,1)}, bf16[320,768]{1,0:T(8,128)(2,1)S(1)}, bf16[320,768]{1,0:T(8,128)(2,1)}) fusion(bf16[256,768]{1,0:T(8,128)(2,1)S(1)} %fusion.86, bf16[128,768]{1,0:T(8,128)(2,1)} %collective-permute-done.4, bf16[128,768]{1,0:T(8,128)(2,1)} %collective-permute-done.9), kind=kLoop, calls=%fused_computation.158 | loop fusion | flops 3932160 | bytes 2752512 | tf_op jit(solution)/shard_map/concatenate | solution.py:25
  (323 shorter events, 85.7 us)
Async XLA Ops:
  2.5 12.5 %copy-start.58 = (f32[768]{0:T(1024)S(1)}, f32[768]{0:T(1024)}, u32[]{:S(2)}) copy-start(f32[768]{0:T(1024)} %param.21) | copy-start | bytes 9220
  4.2 22.0 %copy-start.49 = (s32[256]{0:T(256)S(1)}, s32[256]{0:T(256)}, u32[]{:S(2)}) copy-start(s32[256]{0:T(256)} %param.22) | copy-start | bytes 3076
  4.2 32.6 %copy-start.3 = (bf16[256,768]{1,0:T(8,128)(2,1)S(1)}, bf16[256,768]{1,0:T(8,128)(2,1)}, u32[]{:S(2)}) copy-start(bf16[256,768]{1,0:T(8,128)(2,1)} %param.17) | copy-start | bytes 1179652
  15.9 36.1 %copy-start.59 = (f32[768]{0:T(1024)S(1)}, f32[768]{0:T(1024)}, u32[]{:S(2)}) copy-start(f32[768]{0:T(1024)} %param.18) | copy-start | bytes 9220
  15.9 62.2 %collective-permute-start.4 = (bf16[128,768]{1,0:T(8,128)(2,1)}, bf16[128,768]{1,0:T(8,128)(2,1)}, u32[]{:S(2)}, u32[]{:S(2)}) collective-permute-start(bf16[128,768]{1,0:T(8,128)(2,1)} %get-tuple-element.40), channel_id=1, source_target_pairs={{0,4},{4,8},{8,12},{12,16},{16,20},{20,24},{24,28},{28,32},{32,36}... | collective-permute-start | bytes 589832 | tf_op jit(solution)/shard_map/ppermute | solution.py:23
  18.6 61.5 %collective-permute-start.9 = (bf16[128,768]{1,0:T(8,128)(2,1)}, bf16[128,768]{1,0:T(8,128)(2,1)}, u32[]{:S(2)}, u32[]{:S(2)}) collective-permute-start(bf16[128,768]{1,0:T(8,128)(2,1)} %get-tuple-element.41), channel_id=1, source_target_pairs={{4,0},{8,4},{12,8},{16,12},{20,16},{24,20},{28,24},{32,28},{36,32}... | collective-permute-start | bytes 589832 | tf_op jit(solution)/shard_map/ppermute | solution.py:24
  26.7 39.7 %collective-permute-start.3 = (s32[128]{0:T(128)}, s32[128]{0:T(128)}, u32[]{:S(2)}, u32[]{:S(2)}) collective-permute-start(s32[128]{0:T(128)} %get-tuple-element.56), channel_id=1, source_target_pairs={{0,4},{4,8},{8,12},{12,16},{16,20},{20,24},{24,28},{28,32},{32,36}... | collective-permute-start | bytes 1544 | tf_op jit(solution)/shard_map/ppermute | solution.py:23
  28.7 45.9 %collective-permute-start.8 = (s32[128]{0:T(128)}, s32[128]{0:T(128)}, u32[]{:S(2)}, u32[]{:S(2)}) collective-permute-start(s32[128]{0:T(128)} %get-tuple-element.57), channel_id=1, source_target_pairs={{4,0},{8,4},{12,8},{16,12},{20,16},{24,20},{28,24},{32,28},{36,32}... | collective-permute-start | bytes 1544 | tf_op jit(solution)/shard_map/ppermute | solution.py:24
  37.6 79.0 %collective-permute-start.2 = (bf16[128,768]{1,0:T(8,128)(2,1)}, bf16[128,768]{1,0:T(8,128)(2,1)}, u32[]{:S(2)}, u32[]{:S(2)}) collective-permute-start(bf16[128,768]{1,0:T(8,128)(2,1)} %get-tuple-element.44), channel_id=1, source_target_pairs={{0,4},{4,8},{8,12},{12,16},{16,20},{20,24},{24,28},{28,32},{32,36}... | collective-permute-start | bytes 589832 | tf_op jit(solution)/shard_map/ppermute | solution.py:23
  53.2 38.1 %copy-start.19 = (bf16[128,768]{0,1:T(8,128)(2,1)}, bf16[128,768]{0,1:T(8,128)(2,1)S(1)}, u32[]{:S(2)}) copy-start(bf16[128,768]{0,1:T(8,128)(2,1)S(1)} %get-tuple-element.19) | copy-start | bytes 589828
  56.3 6.3 %copy-start.56 = (s32[320]{0:T(512)S(1)}, s32[320]{0:T(512)}, u32[]{:S(2)}) copy-start(s32[320]{0:T(512)} %iota_add_fusion.2) | copy-start | bytes 3844
  56.4 6.3 %copy-start.84 = (s32[64]{0:T(128)S(1)}, s32[64]{0:T(128)}, u32[]{:S(2)}) copy-start(s32[64]{0:T(128)} %iota_add_fusion.10) | copy-start | bytes 772
  56.4 7.0 %copy-start.57 = (s32[320]{0:T(512)S(1)}, s32[320]{0:T(512)}, u32[]{:S(2)}) copy-start(s32[320]{0:T(512)} %iota_add_fusion.3) | copy-start | bytes 3844
  56.4 7.0 %copy-start.85 = (s32[64]{0:T(128)S(1)}, s32[64]{0:T(128)}, u32[]{:S(2)}) copy-start(s32[64]{0:T(128)} %iota_add_fusion.11) | copy-start | bytes 772
  57.2 6.9 %copy-start.61 = (s32[176]{0:T(256)S(1)}, s32[176]{0:T(256)}, u32[]{:S(2)}) copy-start(s32[176]{0:T(256)} %get-tuple-element.58) | copy-start | bytes 2116
  57.2 6.8 %copy-start.62 = (s32[176]{0:T(256)S(1)}, s32[176]{0:T(256)}, u32[]{:S(2)}) copy-start(s32[176]{0:T(256)} %get-tuple-element.59) | copy-start | bytes 2116
  57.3 7.6 %copy-start.69 = (s32[64]{0:T(128)S(1)}, s32[64]{0:T(128)}, u32[]{:S(2)}) copy-start(s32[64]{0:T(128)} %get-tuple-element.50) | copy-start | bytes 772
  57.3 7.6 %copy-start.70 = (s32[64]{0:T(128)S(1)}, s32[64]{0:T(128)}, u32[]{:S(2)}) copy-start(s32[64]{0:T(128)} %get-tuple-element.51) | copy-start | bytes 772
  57.3 7.6 %copy-start.75 = (pred[384]{0:T(512)(128)(4,1)S(1)}, pred[384]{0:T(512)(128)(4,1)}, u32[]{:S(2)}) copy-start(pred[384]{0:T(512)(128)(4,1)} %compare_and_fusion.7) | copy-start | bytes 1156
  57.3 7.6 %copy-start.77 = (pred[384]{0:T(512)(128)(4,1)S(1)}, pred[384]{0:T(512)(128)(4,1)}, u32[]{:S(2)}) copy-start(pred[384]{0:T(512)(128)(4,1)} %compare_and_fusion.5) | copy-start | bytes 1156
  57.3 8.4 %copy-start.67 = (s32[64]{0:T(128)S(1)}, s32[64]{0:T(128)}, u32[]{:S(2)}) copy-start(s32[64]{0:T(128)} %get-tuple-element.48) | copy-start | bytes 772
  57.3 8.4 %copy-start.68 = (s32[64]{0:T(128)S(1)}, s32[64]{0:T(128)}, u32[]{:S(2)}) copy-start(s32[64]{0:T(128)} %get-tuple-element.49) | copy-start | bytes 772
  57.3 8.3 %copy-start.71 = (pred[384]{0:T(512)(128)(4,1)S(1)}, pred[384]{0:T(512)(128)(4,1)}, u32[]{:S(2)}) copy-start(pred[384]{0:T(512)(128)(4,1)} %compare_and_fusion.11) | copy-start | bytes 1156
  57.3 8.3 %copy-start.73 = (pred[384]{0:T(512)(128)(4,1)S(1)}, pred[384]{0:T(512)(128)(4,1)}, u32[]{:S(2)}) copy-start(pred[384]{0:T(512)(128)(4,1)} %compare_and_fusion.9) | copy-start | bytes 1156
  57.3 20.0 %copy-start.86 = (pred[176]{0:T(512)(128)(4,1)S(1)}, pred[176]{0:T(512)(128)(4,1)}, u32[]{:S(2)}) copy-start(pred[176]{0:T(512)(128)(4,1)} %compare_and_fusion.4) | copy-start | bytes 532
  66.4 66.0 %collective-permute-start.7 = (bf16[128,768]{1,0:T(8,128)(2,1)}, bf16[128,768]{1,0:T(8,128)(2,1)}, u32[]{:S(2)}, u32[]{:S(2)}) collective-permute-start(bf16[128,768]{1,0:T(8,128)(2,1)} %get-tuple-element.45), channel_id=1, source_target_pairs={{4,0},{8,4},{12,8},{16,12},{20,16},{24,20},{28,24},{32,28},{36,32}... | collective-permute-start | bytes 589832 | tf_op jit(solution)/shard_map/ppermute | solution.py:24
  74.6 49.4 %collective-permute-start = (bf16[128,768]{1,0:T(8,128)(2,1)}, bf16[128,768]{1,0:T(8,128)(2,1)}, u32[]{:S(2)}, u32[]{:S(2)}) collective-permute-start(bf16[128,768]{1,0:T(8,128)(2,1)} %get-tuple-element.16), channel_id=1, source_target_pairs={{0,4},{4,8},{8,12},{12,16},{16,20},{20,24},{24,28},{28,32},{32,36}... | collective-permute-start | bytes 589832 | tf_op jit(solution)/shard_map/ppermute | solution.py:23
  78.2 13.4 %collective-permute-start.1 = (bf16[128,768]{0,1:T(8,128)(2,1)S(1)}, bf16[128,768]{0,1:T(8,128)(2,1)S(1)}, u32[]{:S(2)}, u32[]{:S(2)}) collective-permute-start(bf16[128,768]{0,1:T(8,128)(2,1)S(1)} %get-tuple-element.10), channel_id=1, source_target_pairs={{0,4},{4,8},{8,12},{12,16},{16,20},{20,24},{24,28},{28,32},{32,36}... | collective-permute-start | bytes 589832 | tf_op jit(solution)/shard_map/ppermute | solution.py:23
  80.1 15.6 %collective-permute-start.6 = (bf16[128,768]{0,1:T(8,128)(2,1)S(1)}, bf16[128,768]{0,1:T(8,128)(2,1)S(1)}, u32[]{:S(2)}, u32[]{:S(2)}) collective-permute-start(bf16[128,768]{0,1:T(8,128)(2,1)S(1)} %get-tuple-element.11), channel_id=1, source_target_pairs={{4,0},{8,4},{12,8},{16,12},{20,16},{24,20},{28,24},{32,28},{36,32}... | collective-permute-start | bytes 589832 | tf_op jit(solution)/shard_map/ppermute | solution.py:24
  91.6 32.3 %collective-permute-start.5 = (bf16[128,768]{1,0:T(8,128)(2,1)}, bf16[128,768]{1,0:T(8,128)(2,1)}, u32[]{:S(2)}, u32[]{:S(2)}) collective-permute-start(bf16[128,768]{1,0:T(8,128)(2,1)} %get-tuple-element.17), channel_id=1, source_target_pairs={{4,0},{8,4},{12,8},{16,12},{20,16},{24,20},{28,24},{32,28},{36,32}... | collective-permute-start | bytes 589832 | tf_op jit(solution)/shard_map/ppermute | solution.py:24
  162.7 5.7 %copy-start.27 = (bf16[8,6,8,128]{3,2,1,0:T(8,128)(2,1)S(1)}, bf16[8,6,8,128]{3,2,1,0:T(8,128)(2,1)}, u32[]{:S(2)}) copy-start(bf16[8,6,8,128]{3,2,1,0:T(8,128)(2,1)} %get-tuple-element.31) | copy-start | bytes 294916
  162.7 5.7 %copy-start.46 = (pred[64,384]{1,0:T(8,128)(4,1)S(1)}, pred[64,384]{1,0:T(8,128)(4,1)}, u32[]{:S(2)}) copy-start(pred[64,384]{1,0:T(8,128)(4,1)} %get-tuple-element.69) | copy-start | bytes 73732
  (72 other events, 178.9 us)
where the time goes:
time: 200 us; the launch traced here: 198 us
  matrix products  68.8 us (34%)
  starting transfers between devices  46.4 us (23%)
  other arithmetic  35.6 us (18%)
  local copies, waits for them, and re-layouts  35.5 us (18%)
  blocking collectives  10.1 us (5%)
    dot_general x16, matrix products, compute_block_attention(): jnp.einsum('hrk,khe->rhe', probs, values, preferred_element_type=jnp.floa...  38.3 us
    ppermute x5, starting transfers between devices, extended(): after = lax.ppermute(leading, axis, down)  36.1 us
    dot_general x16, matrix products, compute_block_attention(): jnp.einsum('rhe,khe->hrk', query, keys, preferred_element_type=jnp.float32)  15.4 us
    sub x8, matrix products, compute_block_attention(): expo = jnp.exp(scores - top)  15 us
    ppermute x5, starting transfers between devices, extended(): before = lax.ppermute(last, axis, up)  10.3 us
    psum x1, blocking collectives, body(): lax.psum((squares(q_video), squares(k_video), squares(q_audio), squares(k...  10.1 us
    unnamed x193, local copies, waits for them, and re-layouts  8.67 us
    concatenate x4, other arithmetic, extended(): array = jnp.concatenate([before, array, after], axis=dim)  6.79 us
  transfers between devices with their start and end apart: 10, of which 0 were waited for; matrix products, arithmetic and copies ran while one was open for 35% of the time, Pallas kernels for 0%

commit v1 on v0

v1 whole, which is shorter than its diff:
```python
import functools
import math

import jax
import jax.numpy as jnp
from jax import lax
from jax.experimental import pallas as pl
from jax.experimental.pallas import tpu as pltpu
from jax.sharding import PartitionSpec as P

HEAD_DIM = 128
D = 3072
WC = 64
EPS = 1e-06
B = 128
NEG = -1e30
C = math.log2(math.e) / math.sqrt(HEAD_DIM)
MESH = pl.DeviceIdType.MESH
HEADS_AHEAD = 2

ROW_QV, ROW_KV, ROW_QA, ROW_KA, ROW_ALIGN = 0, 4, 8, 10, 12


def dot_nt(a, b):
    return lax.dot_general(a, b, (((1,), (1,)), ((), ())), preferred_element_type=jnp.float32)


def dot_nn(a, b):
    return jnp.dot(a, b, preferred_element_type=jnp.float32)


def with_ones(v):
    return jnp.concatenate([v, jnp.ones(v.shape, v.dtype)], axis=1)


def column(row):
    return jnp.broadcast_to(row, (B, B)).T


def partial_softmax(q, k, v, bias):
    s = dot_nt(q, k) + bias
    m = jnp.max(s, axis=1, keepdims=True)
    p = jnp.exp2((s - m) * C).astype(jnp.bfloat16)
    return m, dot_nn(p, with_ones(v))


def merged(q, k, v, bias, m0, o0):
    s = dot_nt(q, k) + bias
    m1 = jnp.maximum(m0, jnp.max(s, axis=1, keepdims=True))
    p = jnp.exp2((s - m1) * C).astype(jnp.bfloat16)
    a = jnp.exp2((m0 - m1) * C)
    return o0 * jnp.concatenate([a, a], axis=1) + dot_nn(p, with_ones(v))


def ratio(o):
    return o[:, :B] / o[:, B:]


def kernel(
    n_tm, n_head, heads,
    windows, gqv, gkv, gqa, gka, align,
    qv_hbm, kv_hbm, vv_hbm, qa_hbm, ka_hbm, va_hbm,
    ov_hbm, oa_hbm,
    qv, kv, vv, qa, ka, va, halo,
    sums, nb, nbr, fcol, hcol,
    self_bias, va_bias, av_bias, vah_bias, avh_bias,
    qvn, kvn, qan, kan, ms, os, ov, oa,
    load_sem, hsend, hrecv, ssend, srecv, nsend, nrecv, out_sem,
):
    me = lax.axis_index("tm")
    hd = lax.axis_index("head")
    right = lax.rem(me + 1, n_tm)
    left = lax.rem(me + n_tm - 1, n_tm)
    peers = [lax.rem(hd + i, n_head) for i in range(1, n_head)]
    sources = (kv_hbm, vv_hbm, ka_hbm, va_hbm)
    loads = ((qv_hbm, qv), (kv_hbm, kv), (qa_hbm, qa), (ka_hbm, ka), (vv_hbm, vv), (va_hbm, va))

    def columns(h):
        start = h * HEAD_DIM
        return pl.ds(start if isinstance(h, int) else pl.multiple_of(start, HEAD_DIM), HEAD_DIM)

    def load(i, h):
        src, dst = loads[i]
        return pltpu.make_async_copy(src.at[:, columns(h)], dst.at[h], load_sem.at[i, h])

    def halo_copy(h, side, a):
        src = sources[a]
        row = src.shape[0] - B if side == 0 else 0
        return pltpu.make_async_remote_copy(
            src_ref=src.at[pl.ds(row, B), columns(h)],
            dst_ref=halo.at[h, side, a],
            send_sem=hsend.at[h, side, a],
            recv_sem=hrecv.at[h, side, a],
            device_id=(right if side == 0 else left, hd),
            device_id_type=MESH,
        )

    def start_halo(h):
        for a in range(4):
            for side in (0, 1):
                halo_copy(h, side, a).start()

    sums[0] = jnp.zeros((16, B), jnp.float32)
    barrier = pltpu.get_barrier_semaphore()
    for device in [(right, hd), (left, hd)] + [(me, p) for p in peers]:
        pl.semaphore_signal(barrier, inc=1, device_id=device, device_id_type=MESH)
    for i in range(6):
        for h in range(heads):
            load(i, h).start()
    pl.semaphore_wait(barrier, 1 + n_head)
    for h in range(HEADS_AHEAD):
        start_halo(h)

    for i in range(4):
        for h in range(heads):
            load(i, h).wait()
    for ref, row in ((qv, ROW_QV), (kv, ROW_KV), (qa, ROW_QA), (ka, ROW_KA)):
        for r in range(ref.shape[1] // B):
            total = None
            for h in range(heads):
                x = ref[h, r * B : (r + 1) * B, :].astype(jnp.float32)
                total = x * x if total is None else total + x * x
            sums[0, row + r : row + r + 1, :] = jnp.sum(total.T, axis=0, keepdims=True)
    exchange = [
        pltpu.make_async_remote_copy(
            src_ref=sums.at[0],
            dst_ref=sums.at[1 + i],
            send_sem=ssend.at[i],
            recv_sem=srecv.at[i],
            device_id=(me, p),
            device_id_type=MESH,
        )
        for i, p in enumerate(peers)
    ]
    for copy in exchange:
        copy.start()

    v0 = (me * qv.shape[1]).astype(jnp.float32)
    al = align[...].astype(jnp.float32)
    rows = lax.broadcasted_iota(jnp.int32, (B, B), 0)
    cols = lax.broadcasted_iota(jnp.int32, (B, B), 1)
    rowsf = rows.astype(jnp.float32)
    colsf = cols.astype(jnp.float32)

    def near(x, y):
        return jnp.where(jnp.abs(x - y) <= WC, 0.0, NEG).astype(jnp.float32)

    for b in range(4):
        for j in range(2):
            va_bias[b * B : (b + 1) * B, j * B : (j + 1) * B] = near(
                al[j : j + 1, :], rowsf + (v0 + b * B)
            )
    for j in range(2):
        acol = column(al[j : j + 1, :])
        for t in range(3):
            av_bias[j, :, t * B : (t + 1) * B] = near(acol, colsf + (v0 + (j + t) * B))

    for copy in exchange:
        copy.wait()
    total = sums[0]
    for i in range(1, n_head):
        total = total + sums[i]
    nb[...] = lax.rsqrt(total / D + EPS)
    nb[ROW_ALIGN : ROW_ALIGN + 2, :] = al
    to_neighbours = [
        pltpu.make_async_remote_copy(
            src_ref=nb,
            dst_ref=nbr.at[side],
            send_sem=nsend.at[side],
            recv_sem=nrecv.at[side],
            device_id=(right if side == 0 else left, hd),
            device_id_type=MESH,
        )
        for side in (0, 1)
    ]
    for copy in to_neighbours:
        copy.start()
    for c in range(12):
        fcol[c] = column(nb[c : c + 1, :])
    for i in (4, 5):
        for h in range(heads):
            load(i, h).wait()
    no_left = jnp.where(me == 0, NEG, 0.0).astype(jnp.float32)
    no_right = jnp.where(me == n_tm - 1, NEG, 0.0).astype(jnp.float32)
    for copy in to_neighbours:
        copy.wait()
    for side in (0, 1):
        none = no_left if side == 0 else no_right
        rk, ra, rl = ((ROW_KV + 3, ROW_KA + 1, ROW_ALIGN + 1), (ROW_KV, ROW_KA, ROW_ALIGN))[side]
        hcol[side, 0] = column(nbr[side, rk : rk + 1, :])
        hcol[side, 1] = column(nbr[side, ra : ra + 1, :])
        vah_bias[side] = near(nbr[side, rl : rl + 1, :], rowsf + (v0 + 3 * side * B)) + none
        acol = column(al[side : side + 1, :])
        avh_bias[side] = near(acol, colsf + (v0 + (-B if side == 0 else 4 * B))) + none

    def head(h, carry):
        gains = [g[pl.ds(h, 1), :] for g in (gqv, gkv, gqa, gka)]

        def normed(x, factor, gain):
            return (x.astype(jnp.float32) * factor * gain).astype(jnp.bfloat16)

        for src, dst, row, g in (
            (qv, qvn, ROW_QV, 0), (kv, kvn, ROW_KV, 1), (qa, qan, ROW_QA, 2), (ka, kan, ROW_KA, 3),
        ):
            for r in range(src.shape[1] // B):
                part = slice(r * B, (r + 1) * B)
                dst[part, :] = normed(src[h, part, :], fcol[row + r], gains[g])
        for kind in (0, 1):
            w = windows[kind, h]
            for t in range(3):
                far = jnp.abs(cols - rows + (t - 1) * B)
                self_bias[kind, :, t * B : (t + 1) * B] = jnp.where(far <= w, 0.0, NEG).astype(
                    jnp.float32
                )

        def keep(i, m, o):
            ms[i] = jnp.broadcast_to(m, (B, B))
            os[i] = o

        for b in range(4):
            q = qvn[b * B : (b + 1) * B, :]
            lo, hi = max(b - 1, 0), min(b + 2, 4)
            part = slice(lo * B, hi * B)
            bias = self_bias[0, :, (lo - b + 1) * B : (hi - b + 1) * B]
            m_s, o_s = partial_softmax(q, kvn[part, :], vv[h, part, :], bias)
            part = (slice(0, B), slice(0, 2 * B), slice(0, 2 * B), slice(B, 2 * B))[b]
            m_c, o_c = partial_softmax(
                q, kan[part, :], va[h, part, :], va_bias[b * B : (b + 1) * B, part]
            )
            if b in (1, 2):
                ov[h, b * B : (b + 1) * B, :] = (ratio(o_s) + ratio(o_c)).astype(jnp.bfloat16)
            else:
                keep(2 * (b // 3), m_s, o_s)
                keep(2 * (b // 3) + 1, m_c, o_c)
        for j in range(2):
            q = qan[j * B : (j + 1) * B, :]
            bias = self_bias[1, :, (1 - j) * B : (3 - j) * B]
            m_s, o_s = partial_softmax(q, kan[...], va[h], bias)
            part = slice(j * B, (j + 3) * B)
            m_c, o_c = partial_softmax(q, kvn[part, :], vv[h, part, :], av_bias[j])
            keep(4 + 2 * j, m_s, o_s)
            keep(5 + 2 * j, m_c, o_c)

        for a in range(4):
            for side in (0, 1):
                halo_copy(h, side, a).wait()

        @pl.when(h + HEADS_AHEAD < heads)
        def _():
            start_halo(h + HEADS_AHEAD)

        for side in (0, 1):
            none = no_left if side == 0 else no_right
            hk = normed(halo[h, side, 0], hcol[side, 0], gains[1])
            hv = halo[h, side, 1]
            hka = normed(halo[h, side, 2], hcol[side, 1], gains[3])
            hva = halo[h, side, 3]
            b = 3 * side
            part = slice(b * B, (b + 1) * B)
            q = qvn[part, :]
            edge = slice(2 * side * B, (2 * side + 1) * B)
            o_s = merged(q, hk, hv, self_bias[0, :, edge] + none, ms[2 * side], os[2 * side])
            o_c = merged(q, hka, hva, vah_bias[side], ms[2 * side + 1], os[2 * side + 1])
            ov[h, part, :] = (ratio(o_s) + ratio(o_c)).astype(jnp.bfloat16)
            part = slice(side * B, (side + 1) * B)
            q = qan[part, :]
            o_s = merged(q, hka, hva, self_bias[1, :, edge] + none, ms[4 + 2 * side], os[4 + 2 * side])
            o_c = merged(q, hk, hv, avh_bias[side], ms[5 + 2 * side], os[5 + 2 * side])
            oa[h, part, :] = (ratio(o_s) + ratio(o_c)).astype(jnp.bfloat16)
        pltpu.make_async_copy(ov.at[h], ov_hbm.at[:, columns(h)], out_sem.at[0, h]).start()
        pltpu.make_async_copy(oa.at[h], oa_hbm.at[:, columns(h)], out_sem.at[1, h]).start()
        return carry

    lax.fori_loop(0, heads, head, 0)
    for h in range(heads):
        pltpu.make_async_copy(ov.at[h], ov_hbm.at[:, columns(h)], out_sem.at[0, h]).wait()
        pltpu.make_async_copy(oa.at[h], oa_hbm.at[:, columns(h)], out_sem.at[1, h]).wait()


def body(
    q_video, k_video, v_video, q_audio, k_audio, v_audio,
    q_gain_video, k_gain_video, q_gain_audio, k_gain_audio, audio_align, windows,
):
    n_tm, n_head = lax.axis_size("tm"), lax.axis_size("head")
    rows_v, width = q_video.shape
    rows_a = q_audio.shape[0]
    heads = width // HEAD_DIM
    gains = [
        g.reshape(heads, HEAD_DIM) for g in (q_gain_video, k_gain_video, q_gain_audio, k_gain_audio)
    ]
    bf, f32 = jnp.bfloat16, jnp.float32
    vmem = pl.BlockSpec(memory_space=pltpu.VMEM)
    hbm = pl.BlockSpec(memory_space=pltpu.HBM)
    dma = pltpu.SemaphoreType.DMA
    return pl.pallas_call(
        functools.partial(kernel, n_tm, n_head, heads),
        out_shape=(
            jax.ShapeDtypeStruct(q_video.shape, bf),
            jax.ShapeDtypeStruct(q_audio.shape, bf),
        ),
        in_specs=[pl.BlockSpec(memory_space=pltpu.SMEM)] + [vmem] * 5 + [hbm] * 6,
        out_specs=(hbm, hbm),
        scratch_shapes=[
            pltpu.VMEM((heads, rows_v, B), bf),
            pltpu.VMEM((heads, rows_v, B), bf),
            pltpu.VMEM((heads, rows_v, B), bf),
            pltpu.VMEM((heads, rows_a, B), bf),
            pltpu.VMEM((heads, rows_a, B), bf),
            pltpu.VMEM((heads, rows_a, B), bf),
            pltpu.VMEM((heads, 2, 4, B, B), bf),
            pltpu.VMEM((n_head, 16, B), f32),
            pltpu.VMEM((16, B), f32),
            pltpu.VMEM((2, 16, B), f32),
            pltpu.VMEM((12, B, B), f32),
            pltpu.VMEM((2, 2, B, B), f32),
            pltpu.VMEM((2, B, 3 * B), f32),
            pltpu.VMEM((rows_v, rows_a), f32),
            pltpu.VMEM((2, B, 3 * B), f32),
            pltpu.VMEM((2, B, B), f32),
            pltpu.VMEM((2, B, B), f32),
            pltpu.VMEM((rows_v, B), bf),
            pltpu.VMEM((rows_v, B), bf),
            pltpu.VMEM((rows_a, B), bf),
            pltpu.VMEM((rows_a, B), bf),
            pltpu.VMEM((8, B, B), f32),
            pltpu.VMEM((8, B, 2 * B), f32),
            pltpu.VMEM((heads, rows_v, B), bf),
            pltpu.VMEM((heads, rows_a, B), bf),
            dma((6, heads)),
            dma((heads, 2, 4)),
            dma((heads, 2, 4)),
            dma((n_head - 1,)),
            dma((n_head - 1,)),
            dma((2,)),
            dma((2,)),
            dma((2, heads)),
        ],
        compiler_params=pltpu.CompilerParams(
            collective_id=0, has_side_effects=True, vmem_limit_bytes=60 * 2**20
        ),
        name="attention",
    )(
        windows, *gains, audio_align.reshape(rows_a // B, B),
        q_video, k_video, v_video, q_audio, k_audio, v_audio,
    )


def solution(mesh):
    placed = (P("tm", "head"),) * 6 + (P("head"),) * 4 + (P("tm"), P(None, "head"))
    return jax.shard_map(
        body,
        mesh=mesh,
        in_specs=placed,
        out_specs=(P("tm", "head"), P("tm", "head")),
        check_vma=False,
    )
```

time: 200 us -> 61.6 us (0.31)
  the two profiles are of different devices: /device:TPU:256 before, /device:TPU:4 now
where the time goes in v1:
time: 61.6 us; the launch traced here: 61.4 us
  Pallas kernels  57.9 us (94%)
  local copies, waits for them, and re-layouts  2.86 us (5%)
  between operations  0.65 us (1%)
    pallas_call x1, Pallas kernels, body(): pl.pallas_call(functools.partial(kernel, n_tm, n_head, heads), out_shape=...  57.9 us
    unnamed x4, local copies, waits for them, and re-layouts  2.86 us

profile of v1, /device:TPU:4, one launch (start us, length us, event | category | flops | bytes accessed | tf_op | source)
XLA Modules:
  0.0 61.4 jit_solution(9755926103875735385)
XLA Ops:
  0.6 57.9 %attention.1 = (bf16[512,768]{1,0:T(8,128)(2,1)}, bf16[256,768]{1,0:T(8,128)(2,1)}) custom-call(s32[2,6]{1,0:T(2,128)} %windows.1, f32[6,128]{1,0:T(8,128)} %bitcast.5, f32[6,128]{1,0:T(8,128)} %bitcast.6, f32[6,128]{1,0:T(8,128)} %bitcast.7, f32[6,128]{1,0:T(8,128)} %bitcast.8, s32[2,128]{1,0:T(2,128)} %bitcast.9, bf16[512,768]{1,0:T(8,128)(2,1)} %qv_hbm.1, ...), custom_call_target="tpu_custom_call" | custom-call | tf_op jit(solution)/shard_map/attention/pallas_call | solution.py:295
  58.5 0.0 copy-start
  58.5 2.1 %copy.16 = bf16[512,768]{1,0:T(8,128)(2,1)} copy(bf16[512,768]{1,0:T(8,128)(2,1)} %get-tuple-element.4) | data formatting | bytes 1572864
  60.7 0.0 copy-done
  60.7 0.7 %copy.17 = bf16[256,768]{1,0:T(8,128)(2,1)} copy(bf16[256,768]{1,0:T(8,128)(2,1)S(1)} %copy-done) | data formatting | bytes 786432
Async XLA Ops:
  58.5 2.1 %copy-start = (bf16[256,768]{1,0:T(8,128)(2,1)S(1)}, bf16[256,768]{1,0:T(8,128)(2,1)}, u32[]{:S(2)}) copy-start(bf16[256,768]{1,0:T(8,128)(2,1)} %get-tuple-element.5) | copy-start | bytes 1179652

commit v2 on v1

v2 whole, which is shorter than its diff:
```python
import functools
import math

import jax
import jax.numpy as jnp
from jax import lax
from jax.experimental import pallas as pl
from jax.experimental.pallas import tpu as pltpu
from jax.sharding import PartitionSpec as P

HEAD_DIM = 128
D = 3072
WC = 64
EPS = 1e-06
B = 128
NEG = -1e30
C = math.log2(math.e) / math.sqrt(HEAD_DIM)
MESH = pl.DeviceIdType.MESH

ROW_QV, ROW_KV, ROW_QA, ROW_KA, ROW_ALIGN = 0, 4, 8, 10, 12

VIDEO_SELF = ((0, 256), (0, 384), (128, 512), (256, 512))
VIDEO_CROSS = ((0, 96), (0, 160), (64, 224), (128, 256))
AUDIO_SELF = ((0, 256), (0, 256))
AUDIO_CROSS = ((0, 368), (192, 512))
HALO_VIDEO_CROSS = ((64, 128), (0, 32))
HALO_AUDIO_CROSS = ((64, 128), (0, 112))


def dot_nt(a, b):
    return lax.dot_general(a, b, (((1,), (1,)), ((), ())), preferred_element_type=jnp.float32)


def dot_nn(a, b):
    return jnp.dot(a, b, preferred_element_type=jnp.float32)


def column(row):
    return jnp.broadcast_to(row, (B, B)).T


def softened(s):
    m = jnp.max(s, axis=0, keepdims=True)
    e = jnp.exp2((s - m) * C)
    return m, jnp.sum(e, axis=0, keepdims=True), e.astype(jnp.bfloat16)


def padded(p, first, rows):
    last = rows - first - p.shape[0]
    parts = [jnp.zeros((first, B), p.dtype)] if first else []
    parts.append(p)
    if last:
        parts.append(jnp.zeros((last, B), p.dtype))
    return jnp.concatenate(parts, axis=0) if len(parts) > 1 else p


def in_turn(tasks):
    n = len(tasks)
    tasks[0][0]()
    for i in range(n):
        if i + 1 < n:
            tasks[i + 1][0]()
        tasks[i][1]()
        if i > 0:
            tasks[i - 1][2]()
    tasks[n - 1][2]()


def kernel(
    n_tm, n_head, heads,
    windows, gqv, gkv, gqa, gka, align,
    qv_hbm, kv_hbm, vv_hbm, qa_hbm, ka_hbm, va_hbm,
    ov, oa,
    qv, kv, vv, qa, ka, va, halo,
    sums, nb, nbr, fcol, hcol,
    self_bias, va_bias, av_bias, vah_bias, avh_bias,
    qvn, kvn, qan, kan, vvt, vat, qe, ml, os,
    load_sem, hsend, hrecv, ssend, srecv, nsend, nrecv,
):
    me = lax.axis_index("tm")
    hd = lax.axis_index("head")
    right = jnp.minimum(me + 1, n_tm - 1)
    left = jnp.maximum(me - 1, 0)
    has_left = me > 0
    has_right = me < n_tm - 1
    sends_to = (has_right, has_left)
    comes_from = (has_left, has_right)
    peers = [lax.rem(hd + i, n_head) for i in range(1, n_head)]
    sources = (kv_hbm, vv_hbm, ka_hbm, va_hbm)
    loads = ((qv_hbm, qv), (kv_hbm, kv), (qa_hbm, qa), (ka_hbm, ka), (vv_hbm, vv), (va_hbm, va))

    def columns(h):
        start = h * HEAD_DIM
        return pl.ds(start if isinstance(h, int) else pl.multiple_of(start, HEAD_DIM), HEAD_DIM)

    def load(i, h):
        src, dst = loads[i]
        return pltpu.make_async_copy(src.at[:, columns(h)], dst.at[h], load_sem.at[i, h])

    def halo_copy(h, side, a):
        src = sources[a]
        row = src.shape[0] - B if side == 0 else 0
        return pltpu.make_async_remote_copy(
            src_ref=src.at[pl.ds(row, B), columns(h)],
            dst_ref=halo.at[h, side, a],
            send_sem=hsend.at[h, side, a],
            recv_sem=hrecv.at[h, side, a],
            device_id=(right if side == 0 else left, hd),
            device_id_type=MESH,
        )

    def start_halo(h):
        for side in (0, 1):

            @pl.when(sends_to[side])
            def _():
                for a in range(4):
                    halo_copy(h, side, a).start()

    def wait_halo(h):
        for side in (0, 1):

            @pl.when(comes_from[side])
            def _():
                for a in range(4):
                    halo_copy(h, side, a).wait_recv()

    sums[0] = jnp.zeros((16, B), jnp.float32)
    barrier = pltpu.get_barrier_semaphore()
    for p in peers:
        pl.semaphore_signal(barrier, inc=1, device_id=(me, p), device_id_type=MESH)
    for there, device in ((has_right, right), (has_left, left)):

        @pl.when(there)
        def _():
            pl.semaphore_signal(barrier, inc=1, device_id=(device, hd), device_id_type=MESH)

    for i in range(6):
        for h in range(heads):
            load(i, h).start()
    for slot in (0, 1):

        @pl.when(jnp.logical_not(comes_from[slot]))
        def _():
            nbr[slot] = jnp.zeros((16, B), jnp.float32)

            def clear(h, carry):
                halo[h, slot] = jnp.zeros((4, B, B), jnp.bfloat16)
                return carry

            lax.fori_loop(0, heads, clear, 0)

    pl.semaphore_wait(
        barrier, n_head - 1 + has_left.astype(jnp.int32) + has_right.astype(jnp.int32)
    )
    start_halo(0)

    for i in range(4):
        for h in range(heads):
            load(i, h).wait()
    for ref, row in ((qv, ROW_QV), (kv, ROW_KV), (qa, ROW_QA), (ka, ROW_KA)):
        for r in range(ref.shape[1] // B):
            total = None
            for h in range(heads):
                x = ref[h, r * B : (r + 1) * B, :].astype(jnp.float32)
                total = x * x if total is None else total + x * x
            sums[0, row + r : row + r + 1, :] = jnp.sum(total.T, axis=0, keepdims=True)
    exchange = [
        pltpu.make_async_remote_copy(
            src_ref=sums.at[0],
            dst_ref=sums.at[1 + i],
            send_sem=ssend.at[i],
            recv_sem=srecv.at[i],
            device_id=(me, p),
            device_id_type=MESH,
        )
        for i, p in enumerate(peers)
    ]
    for copy in exchange:
        copy.start()
    start_halo(1)
    start_halo(2)

    v0 = (me * qv.shape[1]).astype(jnp.float32)
    al = align[...].astype(jnp.float32)
    rows = lax.broadcasted_iota(jnp.int32, (B, B), 0)
    cols = lax.broadcasted_iota(jnp.int32, (B, B), 1)
    rowsf = rows.astype(jnp.float32)
    colsf = cols.astype(jnp.float32)

    def near(x, y):
        return jnp.where(jnp.abs(x - y) <= WC, 0.0, NEG).astype(jnp.float32)

    acols = [column(al[j : j + 1, :]) for j in range(2)]
    for b, (lo, hi) in enumerate(VIDEO_CROSS):
        for t in range(lo // B, -(-hi // B)):
            first, last = max(lo, t * B), min(hi, (t + 1) * B)
            bias = near(acols[t], colsf + (v0 + b * B))
            va_bias[b, first - lo : last - lo, :] = bias[first - t * B : last - t * B, :]
    for j, (lo, hi) in enumerate(AUDIO_CROSS):
        for t in range(lo // B, -(-hi // B)):
            first, last = max(lo, t * B), min(hi, (t + 1) * B)
            bias = near(al[j : j + 1, :], rowsf + (v0 + t * B))
            av_bias[j, first - lo : last - lo, :] = bias[first - t * B : last - t * B, :]

    for i in (4, 5):
        for h in range(heads):
            load(i, h).wait()

    def turn_values(h, carry):
        for src, dst in ((vv, vvt), (va, vat)):
            for r in range(src.shape[1] // B):
                dst[h, :, r * B : (r + 1) * B] = src[h, r * B : (r + 1) * B, :].T
        return carry

    lax.fori_loop(0, heads, turn_values, 0)

    for copy in exchange:
        copy.wait()
    total = sums[0]
    for i in range(1, n_head):
        total = total + sums[i]
    nb[...] = lax.rsqrt(total / D + EPS)
    nb[ROW_ALIGN : ROW_ALIGN + 2, :] = al
    to_neighbours = [
        pltpu.make_async_remote_copy(
            src_ref=nb,
            dst_ref=nbr.at[side],
            send_sem=nsend.at[side],
            recv_sem=nrecv.at[side],
            device_id=(right if side == 0 else left, hd),
            device_id_type=MESH,
        )
        for side in (0, 1)
    ]
    for side in (0, 1):
        pl.when(sends_to[side])(to_neighbours[side].start)
    for h in range(3, heads):
        start_halo(h)
    for c in range(12):
        fcol[c] = column(nb[c : c + 1, :])
    def normed(x, factor, gain):
        return (x.astype(jnp.float32) * factor * gain).astype(jnp.bfloat16)

    def own_keys(h, carry):
        gains = [g[pl.ds(h, 1), :] for g in (gqv, gkv, gqa, gka)]

        for src, dst, row, g in (
            (qv, qvn, ROW_QV, 0), (kv, kvn, ROW_KV, 1), (qa, qan, ROW_QA, 2), (ka, kan, ROW_KA, 3),
        ):
            for r in range(src.shape[1] // B):
                part = slice(r * B, (r + 1) * B)
                dst[part, :] = normed(src[h, part, :], fcol[row + r], gains[g])
        for kind in (0, 1):
            w = windows[kind, h]
            for t in range(3):
                far = jnp.abs(rows - cols + (t - 1) * B)
                self_bias[h, kind, t * B : (t + 1) * B, :] = jnp.where(far <= w, 0.0, NEG).astype(
                    jnp.float32
                )

        def keep(side, kind, half, m, l, o):
            lanes = slice(half * B, (half + 1) * B)
            row = 4 * side + 2 * kind
            ml[h, row : row + 1, lanes] = m
            ml[h, row + 1 : row + 2, lanes] = l
            os[h, side, kind, :, lanes] = o

        def task(queries, keys, values, windows_of, bias_of, finish):
            lo = min(w[0] for w in windows_of)
            hi = max(w[1] for w in windows_of)
            held = {}

            def scores():
                s = dot_nt(keys[lo:hi, :], queries)
                held["s"] = [
                    s[first - lo : last - lo, i * B : (i + 1) * B]
                    for i, (first, last) in enumerate(windows_of)
                ]

            def weights():
                held["p"] = [softened(held["s"][i] + bias_of(i)) for i in (0, 1)]

            def products():
                p = [
                    padded(held["p"][i][2], windows_of[i][0] - lo, hi - lo) for i in (0, 1)
                ]
                o = dot_nn(values[h, :, lo:hi], jnp.concatenate(p, axis=1))
                finish([(*held["p"][i][:2], o[:, i * B : (i + 1) * B]) for i in (0, 1)])

            return scores, weights, products

        done = {}

        def video_done(pair, kind, results):
            done[pair, kind] = results
            if (pair, 1 - kind) not in done:
                return
            for i in (0, 1):
                b = 2 * pair + i
                if b in (1, 2):
                    o = sum(done[pair, k][i][2] * (1.0 / done[pair, k][i][1]) for k in (0, 1))
                    ov[b * B : (b + 1) * B, columns(h)] = o.astype(jnp.bfloat16).T
                else:
                    for k in (0, 1):
                        keep(pair, k, 0, *done[pair, k][i])

        def audio_done(kind, results):
            for side in (0, 1):
                keep(side, kind, 1, *results[side])

        tasks = []
        for pair in (0, 1):
            q = qvn[2 * pair * B : 2 * (pair + 1) * B, :]
            part = VIDEO_SELF[2 * pair : 2 * pair + 2]

            def self_of(i, pair=pair):
                lo, hi = VIDEO_SELF[2 * pair + i]
                shift = (1 - 2 * pair - i) * B
                return self_bias[h, 0, lo + shift : hi + shift, :]

            tasks.append(
                task(q, kvn, vvt, part, self_of, functools.partial(video_done, pair, 0))
            )
            part = VIDEO_CROSS[2 * pair : 2 * pair + 2]

            def cross_of(i, pair=pair):
                lo, hi = VIDEO_CROSS[2 * pair + i]
                return va_bias[2 * pair + i, 0 : hi - lo, :]

            tasks.append(
                task(q, kan, vat, part, cross_of, functools.partial(video_done, pair, 1))
            )
        tasks.append(
            task(
                qan[...], kvn, vvt, AUDIO_CROSS,
                lambda j: av_bias[j, 0 : AUDIO_CROSS[j][1] - AUDIO_CROSS[j][0], :],
                functools.partial(audio_done, 0),
            )
        )
        tasks.append(
            task(
                qan[...], kan, vat, AUDIO_SELF,
                lambda j: self_bias[h, 1, (1 - j) * B : (3 - j) * B, :],
                functools.partial(audio_done, 1),
            )
        )
        in_turn(tasks)
        for side in (0, 1):
            qe[h, side, :B, :] = qvn[3 * side * B : (3 * side + 1) * B, :]
            qe[h, side, B:, :] = qan[side * B : (side + 1) * B, :]
        return carry

    lax.fori_loop(0, heads, own_keys, 0)

    no_left = jnp.where(me == 0, NEG, 0.0).astype(jnp.float32)
    no_right = jnp.where(me == n_tm - 1, NEG, 0.0).astype(jnp.float32)
    for side in (0, 1):
        pl.when(comes_from[side])(to_neighbours[side].wait_recv)
    for side in (0, 1):
        none = no_left if side == 0 else no_right
        rk, ra, rl = ((ROW_KV + 3, ROW_KA + 1, ROW_ALIGN + 1), (ROW_KV, ROW_KA, ROW_ALIGN))[side]
        hcol[side, 0] = column(nbr[side, rk : rk + 1, :])
        hcol[side, 1] = column(nbr[side, ra : ra + 1, :])
        acol = column(nbr[side, rl : rl + 1, :])
        vah_bias[side] = near(acol, colsf + (v0 + 3 * side * B)) + none
        avh_bias[side] = near(al[side : side + 1, :], rowsf + (v0 + (-B if side == 0 else 4 * B))) + none

    def neighbour_keys(h, carry):
        gains = [g[pl.ds(h, 1), :] for g in (gkv, gka)]
        wait_halo(h)
        total = {}

        def task(side, kind):
            none = no_left if side == 0 else no_right
            edge = slice(2 * side * B, (2 * side + 1) * B)
            reach = (HALO_AUDIO_CROSS, HALO_VIDEO_CROSS)[kind][side]
            cross = (avh_bias, vah_bias)[kind]
            row = 4 * side + 2 * kind
            held = {}

            def scores():
                keys = normed(halo[h, side, 2 * kind], hcol[side, kind], gains[kind])
                held["s"] = dot_nt(keys, qe[h, side])

            def weights():
                results = []
                for i in (0, 1):
                    lanes = slice(i * B, (i + 1) * B)
                    first, last = (0, B) if i == kind else reach
                    if i == kind:
                        bias = self_bias[h, kind, edge, :] + none
                    else:
                        bias = cross[side, first:last, :]
                    s = held["s"][first:last, lanes] + bias
                    m0 = ml[h, row : row + 1, lanes]
                    m = jnp.maximum(m0, jnp.max(s, axis=0, keepdims=True))
                    e = jnp.exp2((s - m) * C)
                    a = jnp.exp2((m0 - m) * C)
                    l = ml[h, row + 1 : row + 2, lanes] * a + jnp.sum(e, axis=0, keepdims=True)
                    results.append((a, l, padded(e.astype(jnp.bfloat16), first, B)))
                held["p"] = results

            def products():
                values = halo[h, side, 2 * kind + 1].T
                o = dot_nn(values, jnp.concatenate([p[2] for p in held["p"]], axis=1))
                for i in (0, 1):
                    lanes = slice(i * B, (i + 1) * B)
                    a, l, _ = held["p"][i]
                    total[kind, i] = (os[h, side, kind, :, lanes] * a + o[:, lanes]) * (1.0 / l)
                if kind == 1:
                    part = slice(3 * side * B, (3 * side + 1) * B)
                    o = total[0, 0] + total[1, 0]
                    ov[part, columns(h)] = o.astype(jnp.bfloat16).T
                    part = slice(side * B, (side + 1) * B)
                    o = total[0, 1] + total[1, 1]
                    oa[part, columns(h)] = o.astype(jnp.bfloat16).T

            return scores, weights, products

        in_turn([task(side, kind) for side in (0, 1) for kind in (0, 1)])
        return carry

    lax.fori_loop(0, heads, neighbour_keys, 0)
    for side in (0, 1):

        @pl.when(sends_to[side])
        def _():
            to_neighbours[side].wait_send()

            def sent(h, carry):
                for a in range(4):
                    halo_copy(h, side, a).wait_send()
                return carry

            lax.fori_loop(0, heads, sent, 0)


def body(
    q_video, k_video, v_video, q_audio, k_audio, v_audio,
    q_gain_video, k_gain_video, q_gain_audio, k_gain_audio, audio_align, windows,
):
    n_tm, n_head = lax.axis_size("tm"), lax.axis_size("head")
    rows_v, width = q_video.shape
    rows_a = q_audio.shape[0]
    heads = width // HEAD_DIM
    gains = [
        g.reshape(heads, HEAD_DIM) for g in (q_gain_video, k_gain_video, q_gain_audio, k_gain_audio)
    ]
    bf, f32 = jnp.bfloat16, jnp.float32
    vmem = pl.BlockSpec(memory_space=pltpu.VMEM)
    hbm = pl.BlockSpec(memory_space=pltpu.HBM)
    dma = pltpu.SemaphoreType.DMA
    return pl.pallas_call(
        functools.partial(kernel, n_tm, n_head, heads),
        out_shape=(
            pltpu.VMEM(q_video.shape, bf),
            pltpu.VMEM(q_audio.shape, bf),
        ),
        in_specs=[pl.BlockSpec(memory_space=pltpu.SMEM)] + [vmem] * 5 + [hbm] * 6,
        out_specs=(vmem, vmem),
        scratch_shapes=[
            pltpu.VMEM((heads, rows_v, B), bf),
            pltpu.VMEM((heads, rows_v, B), bf),
            pltpu.VMEM((heads, rows_v, B), bf),
            pltpu.VMEM((heads, rows_a, B), bf),
            pltpu.VMEM((heads, rows_a, B), bf),
            pltpu.VMEM((heads, rows_a, B), bf),
            pltpu.VMEM((heads, 2, 4, B, B), bf),
            pltpu.VMEM((n_head, 16, B), f32),
            pltpu.VMEM((16, B), f32),
            pltpu.VMEM((2, 16, B), f32),
            pltpu.VMEM((12, B, B), f32),
            pltpu.VMEM((2, 2, B, B), f32),
            pltpu.VMEM((heads, 2, 3 * B, B), f32),
            pltpu.VMEM((4, 160, B), f32),
            pltpu.VMEM((2, 368, B), f32),
            pltpu.VMEM((2, B, B), f32),
            pltpu.VMEM((2, B, B), f32),
            pltpu.VMEM((rows_v, B), bf),
            pltpu.VMEM((rows_v, B), bf),
            pltpu.VMEM((rows_a, B), bf),
            pltpu.VMEM((rows_a, B), bf),
            pltpu.VMEM((heads, B, rows_v), bf),
            pltpu.VMEM((heads, B, rows_a), bf),
            pltpu.VMEM((heads, 2, 2 * B, B), bf),
            pltpu.VMEM((heads, 8, 2 * B), f32),
            pltpu.VMEM((heads, 2, 2, B, 2 * B), f32),
            dma((6, heads)),
            dma((heads, 2, 4)),
            dma((heads, 2, 4)),
            dma((n_head - 1,)),
            dma((n_head - 1,)),
            dma((2,)),
            dma((2,)),
        ],
        compiler_params=pltpu.CompilerParams(
            collective_id=0, has_side_effects=True, vmem_limit_bytes=60 * 2**20
        ),
        name="attention",
    )(
        windows, *gains, audio_align.reshape(rows_a // B, B),
        q_video, k_video, v_video, q_audio, k_audio, v_audio,
    )


def solution(mesh):
    placed = (P("tm", "head"),) * 6 + (P("head"),) * 4 + (P("tm"), P(None, "head"))
    return jax.shard_map(
        body,
        mesh=mesh,
        in_specs=placed,
        out_specs=(P("tm", "head"), P("tm", "head")),
        check_vma=False,
    )
```

time: 61.6 us -> 46.7 us (0.76)
  the two profiles are of different devices: /device:TPU:4 before, /device:TPU:3 now
where the time goes in v2:
time: 46.7 us; the launch traced here: 46.5 us
  Pallas kernels  44.3 us (95%)
  local copies, waits for them, and re-layouts  1.63 us (3%)
  between operations  0.64 us (1%)
    pallas_call x1, Pallas kernels, body(): pl.pallas_call(functools.partial(kernel, n_tm, n_head, heads), out_shape=...  44.3 us
    unnamed x2, local copies, waits for them, and re-layouts  1.63 us

profile of v2, /device:TPU:3, one launch (start us, length us, event | category | flops | bytes accessed | tf_op | source)
XLA Modules:
  0.0 46.5 jit_solution(15343642969729957402)
XLA Ops:
  0.6 44.3 %attention.1 = (bf16[512,768]{1,0:T(8,128)(2,1)S(1)}, bf16[256,768]{1,0:T(8,128)(2,1)S(1)}) custom-call(s32[2,6]{1,0:T(2,128)} %windows.1, f32[6,128]{1,0:T(8,128)} %bitcast.5, f32[6,128]{1,0:T(8,128)} %bitcast.6, f32[6,128]{1,0:T(8,128)} %bitcast.7, f32[6,128]{1,0:T(8,128)} %bitcast.8, s32[2,128]{1,0:T(2,128)} %bitcast.9, bf16[512,768]{1,0:T(8,128)(2,1)} %qv_hbm.1, ...), custom_call_target="tpu_custom_call" | custom-call | tf_op jit(solution)/shard_map/attention/pallas_call | solution.py:454
  44.9 0.9 %copy.16 = bf16[512,768]{1,0:T(8,128)(2,1)} copy(bf16[512,768]{1,0:T(8,128)(2,1)S(1)} %get-tuple-element.2) | data formatting | bytes 1572864
  45.8 0.7 %copy.17 = bf16[256,768]{1,0:T(8,128)(2,1)} copy(bf16[256,768]{1,0:T(8,128)(2,1)S(1)} %get-tuple-element.3) | data formatting | bytes 786432

commit v3 on v2

--- a/solution.py
+++ b/solution.py
@@ -17,7 +17,7 @@
 C = math.log2(math.e) / math.sqrt(HEAD_DIM)
 MESH = pl.DeviceIdType.MESH
 
-ROW_QV, ROW_KV, ROW_QA, ROW_KA, ROW_ALIGN = 0, 4, 8, 10, 12
+ROW_QV, ROW_KV, ROW_QA, ROW_KA = 0, 4, 8, 10
 
 VIDEO_SELF = ((0, 256), (0, 384), (128, 512), (256, 512))
 VIDEO_CROSS = ((0, 96), (0, 160), (64, 224), (128, 256))
@@ -67,15 +67,15 @@
 
 
 def kernel(
-    n_tm, n_head, heads,
-    windows, gqv, gkv, gqa, gka, align,
+    n_tm, heads,
+    windows, gqv_hbm, gkv_hbm, gqa_hbm, gka_hbm, align_hbm,
     qv_hbm, kv_hbm, vv_hbm, qa_hbm, ka_hbm, va_hbm,
     ov, oa,
-    qv, kv, vv, qa, ka, va, halo,
+    gqv, gkv, gqa, gka, align, qv, kv, vv, qa, ka, va, halo,
     sums, nb, nbr, fcol, hcol,
     self_bias, va_bias, av_bias, vah_bias, avh_bias,
     qvn, kvn, qan, kan, vvt, vat, qe, ml, os,
-    load_sem, hsend, hrecv, ssend, srecv, nsend, nrecv,
+    small_sem, load_sem, hsend, hrecv, ssend, srecv, nsend, nrecv,
 ):
     me = lax.axis_index("tm")
     hd = lax.axis_index("head")
@@ -85,7 +85,7 @@
     has_right = me < n_tm - 1
     sends_to = (has_right, has_left)
     comes_from = (has_left, has_right)
-    peers = [lax.rem(hd + i, n_head) for i in range(1, n_head)]
+    peers = [lax.bitwise_xor(hd, 1), lax.bitwise_xor(hd, 2)]
     sources = (kv_hbm, vv_hbm, ka_hbm, va_hbm)
     loads = ((qv_hbm, qv), (kv_hbm, kv), (qa_hbm, qa), (ka_hbm, ka), (vv_hbm, vv), (va_hbm, va))
 
@@ -96,6 +96,13 @@
     def load(i, h):
         src, dst = loads[i]
         return pltpu.make_async_copy(src.at[:, columns(h)], dst.at[h], load_sem.at[i, h])
+
+    small = [
+        pltpu.make_async_copy(src, dst, small_sem.at[i])
+        for i, (src, dst) in enumerate(
+            ((align_hbm, align), (gqv_hbm, gqv), (gkv_hbm, gkv), (gqa_hbm, gqa), (gka_hbm, gka))
+        )
+    ]
 
     def halo_copy(h, side, a):
         src = sources[a]
@@ -109,23 +116,32 @@
             device_id_type=MESH,
         )
 
-    def start_halo(h):
+    def start_halo(h, kinds=(0, 1)):
+        for kind in kinds:
+            for side in (0, 1):
+
+                @pl.when(sends_to[side])
+                def _():
+                    for a in (2 * kind, 2 * kind + 1):
+                        halo_copy(h, side, a).start()
+
+    def wait_halo(h, kind):
         for side in (0, 1):
 
             @pl.when(sends_to[side])
             def _():
-                for a in range(4):
-                    halo_copy(h, side, a).start()
-
-    def wait_halo(h):
+                for a in (2 * kind, 2 * kind + 1):
+                    halo_copy(h, side, a).wait_send()
+
         for side in (0, 1):
 
             @pl.when(comes_from[side])
             def _():
-                for a in range(4):
+                for a in (2 * kind, 2 * kind + 1):
                     halo_copy(h, side, a).wait_recv()
 
     sums[0] = jnp.zeros((16, B), jnp.float32)
+    nb[...] = jnp.zeros_like(nb)
     barrier = pltpu.get_barrier_semaphore()
     for p in peers:
         pl.semaphore_signal(barrier, inc=1, device_id=(me, p), device_id_type=MESH)
@@ -135,14 +151,19 @@
         def _():
             pl.semaphore_signal(barrier, inc=1, device_id=(device, hd), device_id_type=MESH)
 
-    for i in range(6):
+    for i in range(4):
+        for h in range(heads):
+            load(i, h).start()
+    for copy in small:
+        copy.start()
+    for i in (4, 5):
         for h in range(heads):
             load(i, h).start()
     for slot in (0, 1):
 
         @pl.when(jnp.logical_not(comes_from[slot]))
         def _():
-            nbr[slot] = jnp.zeros((16, B), jnp.float32)
+            nbr[slot] = jnp.zeros((8, B), jnp.float32)
 
             def clear(h, carry):
                 halo[h, slot] = jnp.zeros((4, B, B), jnp.bfloat16)
@@ -151,9 +172,9 @@
             lax.fori_loop(0, heads, clear, 0)
 
     pl.semaphore_wait(
-        barrier, n_head - 1 + has_left.astype(jnp.int32) + has_right.astype(jnp.int32)
+        barrier, 2 + has_left.astype(jnp.int32) + has_right.astype(jnp.int32)
     )
-    start_halo(0)
+    start_halo(0, (0,))
 
     for i in range(4):
         for h in range(heads):
@@ -167,8 +188,8 @@
             sums[0, row + r : row + r + 1, :] = jnp.sum(total.T, axis=0, keepdims=True)
     exchange = [
         pltpu.make_async_remote_copy(
-            src_ref=sums.at[0],
-            dst_ref=sums.at[1 + i],
+            src_ref=sums.at[2 * i],
+            dst_ref=sums.at[2 * i + 1],
             send_sem=ssend.at[i],
             recv_sem=srecv.at[i],
             device_id=(me, p),
@@ -176,11 +197,11 @@
         )
         for i, p in enumerate(peers)
     ]
-    for copy in exchange:
-        copy.start()
-    start_halo(1)
-    start_halo(2)
-
+    exchange[0].start()
+    start_halo(0, (1,))
+
+    for copy in small:
+        copy.wait()
     v0 = (me * qv.shape[1]).astype(jnp.float32)
     al = align[...].astype(jnp.float32)
     rows = lax.broadcasted_iota(jnp.int32, (B, B), 0)
@@ -207,6 +228,12 @@
         for h in range(heads):
             load(i, h).wait()
 
+    exchange[0].wait()
+    sums[2] = sums[0] + sums[1]
+    exchange[1].start()
+    start_halo(1)
+    start_halo(2)
+
     def turn_values(h, carry):
         for src, dst in ((vv, vvt), (va, vat)):
             for r in range(src.shape[1] // B):
@@ -215,16 +242,15 @@
 
     lax.fori_loop(0, heads, turn_values, 0)
 
-    for copy in exchange:
-        copy.wait()
-    total = sums[0]
-    for i in range(1, n_head):
-        total = total + sums[i]
-    nb[...] = lax.rsqrt(total / D + EPS)
-    nb[ROW_ALIGN : ROW_ALIGN + 2, :] = al
+    exchange[1].wait()
+    factors = lax.rsqrt((sums[2] + sums[3]) / D + EPS)
+    for side, picked in enumerate(((ROW_KV + 3, ROW_KA + 1, 1), (ROW_KV, ROW_KA, 0))):
+        for i, row in enumerate(picked):
+            source = factors if i < 2 else al
+            nb[side, i : i + 1, :] = source[row : row + 1, :]
     to_neighbours = [
         pltpu.make_async_remote_copy(
-            src_ref=nb,
+            src_ref=nb.at[side],
             dst_ref=nbr.at[side],
             send_sem=nsend.at[side],
             recv_sem=nrecv.at[side],
@@ -238,7 +264,8 @@
     for h in range(3, heads):
         start_halo(h)
     for c in range(12):
-        fcol[c] = column(nb[c : c + 1, :])
+        fcol[c] = column(factors[c : c + 1, :])
+
     def normed(x, factor, gain):
         return (x.astype(jnp.float32) * factor * gain).astype(jnp.bfloat16)
 
@@ -359,16 +386,17 @@
         pl.when(comes_from[side])(to_neighbours[side].wait_recv)
     for side in (0, 1):
         none = no_left if side == 0 else no_right
-        rk, ra, rl = ((ROW_KV + 3, ROW_KA + 1, ROW_ALIGN + 1), (ROW_KV, ROW_KA, ROW_ALIGN))[side]
-        hcol[side, 0] = column(nbr[side, rk : rk + 1, :])
-        hcol[side, 1] = column(nbr[side, ra : ra + 1, :])
-        acol = column(nbr[side, rl : rl + 1, :])
+        hcol[side, 0] = column(nbr[side, 0:1, :])
+        hcol[side, 1] = column(nbr[side, 1:2, :])
+        acol = column(nbr[side, 2:3, :])
         vah_bias[side] = near(acol, colsf + (v0 + 3 * side * B)) + none
         avh_bias[side] = near(al[side : side + 1, :], rowsf + (v0 + (-B if side == 0 else 4 * B))) + none
 
+    for side in (0, 1):
+        pl.when(sends_to[side])(to_neighbours[side].wait_send)
+
     def neighbour_keys(h, carry):
         gains = [g[pl.ds(h, 1), :] for g in (gkv, gka)]
-        wait_halo(h)
         total = {}
 
         def task(side, kind):
@@ -408,39 +436,53 @@
                     lanes = slice(i * B, (i + 1) * B)
                     a, l, _ = held["p"][i]
                     total[kind, i] = (os[h, side, kind, :, lanes] * a + o[:, lanes]) * (1.0 / l)
+                    if kind == 0:
+                        os[h, side, kind, :, lanes] = total[kind, i]
                 if kind == 1:
+                    o = [os[h, side, 0, :, i * B : (i + 1) * B] + total[1, i] for i in (0, 1)]
                     part = slice(3 * side * B, (3 * side + 1) * B)
-                    o = total[0, 0] + total[1, 0]
-                    ov[part, columns(h)] = o.astype(jnp.bfloat16).T
+                    ov[part, columns(h)] = o[0].astype(jnp.bfloat16).T
                     part = slice(side * B, (side + 1) * B)
-                    o = total[0, 1] + total[1, 1]
-                    oa[part, columns(h)] = o.astype(jnp.bfloat16).T
+                    oa[part, columns(h)] = o[1].astype(jnp.bfloat16).T
 
             return scores, weights, products
 
-        in_turn([task(side, kind) for side in (0, 1) for kind in (0, 1)])
+        for kind in (0, 1):
+            wait_halo(h, kind)
+            in_turn([task(side, kind) for side in (0, 1)])
         return carry
 
     lax.fori_loop(0, heads, neighbour_keys, 0)
-    for side in (0, 1):
-
-        @pl.when(sends_to[side])
-        def _():
-            to_neighbours[side].wait_send()
-
-            def sent(h, carry):
-                for a in range(4):
-                    halo_copy(h, side, a).wait_send()
-                return carry
-
-            lax.fori_loop(0, heads, sent, 0)
+
+
+def move_kernel(a, b, x, y, sems):
+    copies = [
+        pltpu.make_async_copy(src, dst, sems.at[i]) for i, (src, dst) in enumerate(((a, x), (b, y)))
+    ]
+    for copy in copies:
+        copy.start()
+    for copy in copies:
+        copy.wait()
+
+
+def moved(arrays):
+    vmem = pl.BlockSpec(memory_space=pltpu.VMEM)
+    hbm = pl.BlockSpec(memory_space=pltpu.HBM)
+    return pl.pallas_call(
+        move_kernel,
+        out_shape=tuple(jax.ShapeDtypeStruct(x.shape, x.dtype) for x in arrays),
+        in_specs=[vmem, vmem],
+        out_specs=(hbm, hbm),
+        scratch_shapes=[pltpu.SemaphoreType.DMA((2,))],
+        name="moved",
+    )(*[pltpu.with_memory_space_constraint(x, pltpu.VMEM) for x in arrays])
 
 
 def body(
     q_video, k_video, v_video, q_audio, k_audio, v_audio,
     q_gain_video, k_gain_video, q_gain_audio, k_gain_audio, audio_align, windows,
 ):
-    n_tm, n_head = lax.axis_size("tm"), lax.axis_size("head")
+    n_tm = lax.axis_size("tm")
     rows_v, width = q_video.shape
     rows_a = q_audio.shape[0]
     heads = width // HEAD_DIM
@@ -451,15 +493,17 @@
     vmem = pl.BlockSpec(memory_space=pltpu.VMEM)
     hbm = pl.BlockSpec(memory_space=pltpu.HBM)
     dma = pltpu.SemaphoreType.DMA
-    return pl.pallas_call(
-        functools.partial(kernel, n_tm, n_head, heads),
+    results = pl.pallas_call(
+        functools.partial(kernel, n_tm, heads),
         out_shape=(
             pltpu.VMEM(q_video.shape, bf),
             pltpu.VMEM(q_audio.shape, bf),
         ),
-        in_specs=[pl.BlockSpec(memory_space=pltpu.SMEM)] + [vmem] * 5 + [hbm] * 6,
+        in_specs=[pl.BlockSpec(memory_space=pltpu.SMEM)] + [hbm] * 11,
         out_specs=(vmem, vmem),
         scratch_shapes=[
+            *[pltpu.VMEM((heads, B), f32) for _ in range(4)],
+            pltpu.VMEM((rows_a // B, B), jnp.int32),
             pltpu.VMEM((heads, rows_v, B), bf),
             pltpu.VMEM((heads, rows_v, B), bf),
             pltpu.VMEM((heads, rows_v, B), bf),
@@ -467,9 +511,9 @@
             pltpu.VMEM((heads, rows_a, B), bf),
             pltpu.VMEM((heads, rows_a, B), bf),
             pltpu.VMEM((heads, 2, 4, B, B), bf),
-            pltpu.VMEM((n_head, 16, B), f32),
-            pltpu.VMEM((16, B), f32),
-            pltpu.VMEM((2, 16, B), f32),
+            pltpu.VMEM((4, 16, B), f32),
+            pltpu.VMEM((2, 8, B), f32),
+            pltpu.VMEM((2, 8, B), f32),
             pltpu.VMEM((12, B, B), f32),
             pltpu.VMEM((2, 2, B, B), f32),
             pltpu.VMEM((heads, 2, 3 * B, B), f32),
@@ -486,11 +530,12 @@
             pltpu.VMEM((heads, 2, 2 * B, B), bf),
             pltpu.VMEM((heads, 8, 2 * B), f32),
             pltpu.VMEM((heads, 2, 2, B, 2 * B), f32),
+            dma((5,)),
             dma((6, heads)),
             dma((heads, 2, 4)),
             dma((heads, 2, 4)),
-            dma((n_head - 1,)),
-            dma((n_head - 1,)),
+            dma((2,)),
+            dma((2,)),
             dma((2,)),
             dma((2,)),
         ],
@@ -502,6 +547,7 @@
         windows, *gains, audio_align.reshape(rows_a // B, B),
         q_video, k_video, v_video, q_audio, k_audio, v_audio,
     )
+    return moved(results)
 
 
 def solution(mesh):

time: 46.7 us -> 45.3 us (0.970)
  local copies, waits for them, and re-layouts: 1.63 us -> 0 us
    unnamed x2 -> x0, local copies, waits for them, and re-layouts: 1.63 us -> none
    pallas_call x1 -> x2, Pallas kernels: 44.3 us -> 44.5 us  [the longest x1 43.5 us: body(): pl.pallas_call(functools.partial(kernel, n_tm, heads), out_shape=(pltpu.V...]
where the time goes in v3:
time: 45.3 us; the launch traced here: 45.1 us
  Pallas kernels  44.5 us (98%)
  between operations  0.64 us (1%)
    pallas_call x1, Pallas kernels, body(): pl.pallas_call(functools.partial(kernel, n_tm, heads), out_shape=(pltpu.V...  43.5 us
    pallas_call x1, Pallas kernels, moved(): pl.pallas_call(move_kernel, out_shape=tuple((jax.ShapeDtypeStruct(x.shape...  1.02 us

profile of v3, /device:TPU:3, one launch (start us, length us, event | category | flops | bytes accessed | tf_op | source)
XLA Modules:
  0.0 45.1 jit_solution(4592628783716780235)
XLA Ops:
  0.6 43.5 %attention.1 = (bf16[512,768]{1,0:T(8,128)(2,1)S(1)}, bf16[256,768]{1,0:T(8,128)(2,1)S(1)}) custom-call(s32[2,6]{1,0:T(2,128)} %windows.1, f32[6,128]{1,0:T(8,128)} %bitcast.5, f32[6,128]{1,0:T(8,128)} %bitcast.6, f32[6,128]{1,0:T(8,128)} %bitcast.7, f32[6,128]{1,0:T(8,128)} %bitcast.8, s32[2,128]{1,0:T(2,128)} %bitcast.9, bf16[512,768]{1,0:T(8,128)(2,1)} %qv_hbm.1, ...), custom_call_target="tpu_custom_call" | custom-call | tf_op jit(solution)/shard_map/attention/pallas_call | solution.py:496
  44.1 1.0 %moved.1 = (bf16[512,768]{1,0:T(8,128)(2,1)}, bf16[256,768]{1,0:T(8,128)(2,1)}) custom-call(bf16[512,768]{1,0:T(8,128)(2,1)S(1)} %get-tuple-element.4.a, bf16[256,768]{1,0:T(8,128)(2,1)S(1)} %get-tuple-element.5.b), custom_call_target="tpu_custom_call" | custom-call | tf_op jit(solution)/shard_map/moved/pallas_call | solution.py:471

commit v4 on v3

--- a/solution.py
+++ b/solution.py
@@ -68,10 +68,10 @@
 
 def kernel(
     n_tm, heads,
-    windows, gqv_hbm, gkv_hbm, gqa_hbm, gka_hbm, align_hbm,
+    windows_hbm, gqv_hbm, gkv_hbm, gqa_hbm, gka_hbm, align_hbm,
     qv_hbm, kv_hbm, vv_hbm, qa_hbm, ka_hbm, va_hbm,
     ov, oa,
-    gqv, gkv, gqa, gka, align, qv, kv, vv, qa, ka, va, halo,
+    windows, gqv, gkv, gqa, gka, align, qv, kv, vv, qa, ka, va, halo,
     sums, nb, nbr, fcol, hcol,
     self_bias, va_bias, av_bias, vah_bias, avh_bias,
     qvn, kvn, qan, kan, vvt, vat, qe, ml, os,
@@ -100,7 +100,8 @@
     small = [
         pltpu.make_async_copy(src, dst, small_sem.at[i])
         for i, (src, dst) in enumerate(
-            ((align_hbm, align), (gqv_hbm, gqv), (gkv_hbm, gkv), (gqa_hbm, gqa), (gka_hbm, gka))
+            ((align_hbm, align), (gqv_hbm, gqv), (gkv_hbm, gkv), (gqa_hbm, gqa), (gka_hbm, gka),
+             (windows_hbm, windows))
         )
     ]
 
@@ -499,9 +500,10 @@
             pltpu.VMEM(q_video.shape, bf),
             pltpu.VMEM(q_audio.shape, bf),
         ),
-        in_specs=[pl.BlockSpec(memory_space=pltpu.SMEM)] + [hbm] * 11,
+        in_specs=[hbm] * 12,
         out_specs=(vmem, vmem),
         scratch_shapes=[
+            pltpu.SMEM(windows.shape, jnp.int32),
             *[pltpu.VMEM((heads, B), f32) for _ in range(4)],
             pltpu.VMEM((rows_a // B, B), jnp.int32),
             pltpu.VMEM((heads, rows_v, B), bf),
@@ -530,7 +532,7 @@
             pltpu.VMEM((heads, 2, 2 * B, B), bf),
             pltpu.VMEM((heads, 8, 2 * B), f32),
             pltpu.VMEM((heads, 2, 2, B, 2 * B), f32),
-            dma((5,)),
+            dma((6,)),
             dma((6, heads)),
             dma((heads, 2, 4)),
             dma((heads, 2, 4)),

time: 45.3 us -> 44.6 us (0.985)
  Pallas kernels: 44.5 us -> 43.8 us
    pallas_call x1, Pallas kernels: 43.5 us -> 42.8 us  [body(): pl.pallas_call(functools.partial(kernel, n_tm, heads), out_shape=(pltpu.V...]
where the time goes in v4:
time: 44.6 us; the launch traced here: 44.5 us
  Pallas kernels  43.8 us (98%)
  between operations  0.64 us (1%)
    pallas_call x1, Pallas kernels, body(): pl.pallas_call(functools.partial(kernel, n_tm, heads), out_shape=(pltpu.V...  42.8 us
    pallas_call x1, Pallas kernels, moved(): pl.pallas_call(move_kernel, out_shape=tuple((jax.ShapeDtypeStruct(x.shape...  1.02 us

profile of v4, /device:TPU:3, one launch (start us, length us, event | category | flops | bytes accessed | tf_op | source)
XLA Modules:
  0.0 44.5 jit_solution(14506404358091947351)
XLA Ops:
  0.6 42.8 %attention.1 = (bf16[512,768]{1,0:T(8,128)(2,1)S(1)}, bf16[256,768]{1,0:T(8,128)(2,1)S(1)}) custom-call(s32[2,6]{1,0:T(2,128)} %windows_hbm.1, f32[6,128]{1,0:T(8,128)} %bitcast.5, f32[6,128]{1,0:T(8,128)} %bitcast.6, f32[6,128]{1,0:T(8,128)} %bitcast.7, f32[6,128]{1,0:T(8,128)} %bitcast.8, s32[2,128]{1,0:T(2,128)} %bitcast.9, bf16[512,768]{1,0:T(8,128)(2,1)} %qv_hbm.1, ...), custom_call_target="tpu_custom_call" | custom-call | tf_op jit(solution)/shard_map/attention/pallas_call | solution.py:497
  43.4 1.0 %moved.1 = (bf16[512,768]{1,0:T(8,128)(2,1)}, bf16[256,768]{1,0:T(8,128)(2,1)}) custom-call(bf16[512,768]{1,0:T(8,128)(2,1)S(1)} %get-tuple-element.4.a, bf16[256,768]{1,0:T(8,128)(2,1)S(1)} %get-tuple-element.5.b), custom_call_target="tpu_custom_call" | custom-call | tf_op jit(solution)/shard_map/moved/pallas_call | solution.py:472

commit v5 on v4

--- a/solution.py
+++ b/solution.py
@@ -119,27 +119,15 @@
 
     def start_halo(h, kinds=(0, 1)):
         for kind in kinds:
-            for side in (0, 1):
-
-                @pl.when(sends_to[side])
-                def _():
-                    for a in (2 * kind, 2 * kind + 1):
-                        halo_copy(h, side, a).start()
-
-    def wait_halo(h, kind):
+            for a in (2 * kind, 2 * kind + 1):
+                for side in (0, 1):
+                    pl.when(sends_to[side])(halo_copy(h, side, a).start)
+
+    def wait_halo(h, a):
         for side in (0, 1):
-
-            @pl.when(sends_to[side])
-            def _():
-                for a in (2 * kind, 2 * kind + 1):
-                    halo_copy(h, side, a).wait_send()
-
+            pl.when(sends_to[side])(halo_copy(h, side, a).wait_send)
         for side in (0, 1):
-
-            @pl.when(comes_from[side])
-            def _():
-                for a in (2 * kind, 2 * kind + 1):
-                    halo_copy(h, side, a).wait_recv()
+            pl.when(comes_from[side])(halo_copy(h, side, a).wait_recv)
 
     sums[0] = jnp.zeros((16, B), jnp.float32)
     nb[...] = jnp.zeros_like(nb)
@@ -449,8 +437,14 @@
             return scores, weights, products
 
         for kind in (0, 1):
-            wait_halo(h, kind)
-            in_turn([task(side, kind) for side in (0, 1)])
+            tasks = [task(side, kind) for side in (0, 1)]
+            wait_halo(h, 2 * kind)
+            for step in (0, 1):
+                for steps in tasks:
+                    steps[step]()
+            wait_halo(h, 2 * kind + 1)
+            for steps in tasks:
+                steps[2]()
         return carry
 
     lax.fori_loop(0, heads, neighbour_keys, 0)

time: 44.6 us -> 44.5 us (level)
  no operation moved by 1% of the time
where the time goes in v5:
time: 44.5 us; the launch traced here: 44.3 us
  Pallas kernels  43.6 us (98%)
  between operations  0.64 us (1%)
    pallas_call x1, Pallas kernels, body(): pl.pallas_call(functools.partial(kernel, n_tm, heads), out_shape=(pltpu.V...  42.6 us
    pallas_call x1, Pallas kernels, moved(): pl.pallas_call(move_kernel, out_shape=tuple((jax.ShapeDtypeStruct(x.shape...  1.02 us

profile of v5, /device:TPU:3, one launch (start us, length us, event | category | flops | bytes accessed | tf_op | source)
XLA Modules:
  0.0 44.3 jit_solution(4568599096048702596)
XLA Ops:
  0.6 42.6 %attention.1 = (bf16[512,768]{1,0:T(8,128)(2,1)S(1)}, bf16[256,768]{1,0:T(8,128)(2,1)S(1)}) custom-call(s32[2,6]{1,0:T(2,128)} %windows_hbm.1, f32[6,128]{1,0:T(8,128)} %bitcast.5, f32[6,128]{1,0:T(8,128)} %bitcast.6, f32[6,128]{1,0:T(8,128)} %bitcast.7, f32[6,128]{1,0:T(8,128)} %bitcast.8, s32[2,128]{1,0:T(2,128)} %bitcast.9, bf16[512,768]{1,0:T(8,128)(2,1)} %qv_hbm.1, ...), custom_call_target="tpu_custom_call" | custom-call | tf_op jit(solution)/shard_map/attention/pallas_call | solution.py:491
  43.3 1.0 %moved.1 = (bf16[512,768]{1,0:T(8,128)(2,1)}, bf16[256,768]{1,0:T(8,128)(2,1)}) custom-call(bf16[512,768]{1,0:T(8,128)(2,1)S(1)} %get-tuple-element.4.a, bf16[256,768]{1,0:T(8,128)(2,1)S(1)} %get-tuple-element.5.b), custom_call_target="tpu_custom_call" | custom-call | tf_op jit(solution)/shard_map/moved/pallas_call | solution.py:466

commit v6 on v5

--- a/solution.py
+++ b/solution.py
@@ -143,27 +143,27 @@
     for i in range(4):
         for h in range(heads):
             load(i, h).start()
+    for slot in (0, 1):
+
+        @pl.when(jnp.logical_not(comes_from[slot]))
+        def _():
+            nbr[slot] = jnp.zeros((8, B), jnp.float32)
+
+            def clear(h, carry):
+                halo[h, slot] = jnp.zeros((4, B, B), jnp.bfloat16)
+                return carry
+
+            lax.fori_loop(0, heads, clear, 0)
+
+    pl.semaphore_wait(
+        barrier, 2 + has_left.astype(jnp.int32) + has_right.astype(jnp.int32)
+    )
+    start_halo(0, (0,))
     for copy in small:
         copy.start()
     for i in (4, 5):
         for h in range(heads):
             load(i, h).start()
-    for slot in (0, 1):
-
-        @pl.when(jnp.logical_not(comes_from[slot]))
-        def _():
-            nbr[slot] = jnp.zeros((8, B), jnp.float32)
-
-            def clear(h, carry):
-                halo[h, slot] = jnp.zeros((4, B, B), jnp.bfloat16)
-                return carry
-
-            lax.fori_loop(0, heads, clear, 0)
-
-    pl.semaphore_wait(
-        barrier, 2 + has_left.astype(jnp.int32) + has_right.astype(jnp.int32)
-    )
-    start_halo(0, (0,))
 
     for i in range(4):
         for h in range(heads):

time: 44.5 us -> 44.5 us (level)
  the two profiles are of different devices: /device:TPU:3 before, /device:TPU:448 now
where the time goes in v6:
time: 44.5 us; the launch traced here: 44.4 us
  Pallas kernels  43.7 us (98%)
  between operations  0.64 us (1%)
    pallas_call x1, Pallas kernels, body(): pl.pallas_call(functools.partial(kernel, n_tm, heads), out_shape=(pltpu.V...  42.7 us
    pallas_call x1, Pallas kernels, moved(): pl.pallas_call(move_kernel, out_shape=tuple((jax.ShapeDtypeStruct(x.shape...  1.02 us

profile of v6, /device:TPU:448, one launch (start us, length us, event | category | flops | bytes accessed | tf_op | source)
XLA Modules:
  0.0 44.4 jit_solution(8206269454030915385)
XLA Ops:
  0.6 42.7 %attention.1 = (bf16[512,768]{1,0:T(8,128)(2,1)S(1)}, bf16[256,768]{1,0:T(8,128)(2,1)S(1)}) custom-call(s32[2,6]{1,0:T(2,128)} %windows_hbm.1, f32[6,128]{1,0:T(8,128)} %bitcast.5, f32[6,128]{1,0:T(8,128)} %bitcast.6, f32[6,128]{1,0:T(8,128)} %bitcast.7, f32[6,128]{1,0:T(8,128)} %bitcast.8, s32[2,128]{1,0:T(2,128)} %bitcast.9, bf16[512,768]{1,0:T(8,128)(2,1)} %qv_hbm.1, ...), custom_call_target="tpu_custom_call" | custom-call | tf_op jit(solution)/shard_map/attention/pallas_call | solution.py:491
  43.4 1.0 %moved.1 = (bf16[512,768]{1,0:T(8,128)(2,1)}, bf16[256,768]{1,0:T(8,128)(2,1)}) custom-call(bf16[512,768]{1,0:T(8,128)(2,1)S(1)} %get-tuple-element.4.a, bf16[256,768]{1,0:T(8,128)(2,1)S(1)} %get-tuple-element.5.b), custom_call_target="tpu_custom_call" | custom-call | tf_op jit(solution)/shard_map/moved/pallas_call | solution.py:466
